TPU v7x, 32 devices: a whole 2x2x4 slice. The times are simulated.
32 devices in a mesh: dp: 8 (over z, y), seq: 4 (over x, core).
Axes of the slice: x: 2, y: 2, z: 4, core: 2. Of those that a mesh axis runs over, the one named last changes fastest.
Arguments:
- tokens: bfloat16 [32, 576, 768], P('dp', 'seq'), may hold values from -6 to 6
- cotangent: bfloat16 [32, 576, 768], P('dp', 'seq'), may hold values from -6 to 6
- pad_mask: int32 [32, 576], P('dp', 'seq'), may hold values from 0 to 1, as said below
- expert_ids: int32 [32, 576, 2], P('dp', 'seq'), may hold values from 0 to 7, all different within a row
- priority: int32 [32, 576], P('dp', 'seq'), may hold values from 0 to 575, as said below
- ln1_gain: bfloat16 [768], P(('dp', 'seq')), may hold values from 0.5 to 1.5
- ln1_shift: bfloat16 [768], P(('dp', 'seq')), may hold values from -1.25 to 1.25
- w_qkv: bfloat16 [768, 2304], P(('dp', 'seq')), may hold values from -0.3125 to 0.3125
- w_out: bfloat16 [768, 768], P(('dp', 'seq')), may hold values from -0.875 to 0.875
- out_bias: bfloat16 [768], P(('dp', 'seq')), may hold values from -0.625 to 0.625
- ln2_gain: bfloat16 [768], P(('dp', 'seq')), may hold values from 0.5 to 1.5
- ln2_shift: bfloat16 [768], P(('dp', 'seq')), may hold values from -1.25 to 1.25
- w_router: bfloat16 [768, 8], P(('dp', 'seq')), may hold values from -0.15625 to 0.15625
- w_in: bfloat16 [8, 768, 3072], P('dp', None, 'seq'), may hold values from -0.21875 to 0.21875
- in_bias: bfloat16 [8, 3072], P('dp', 'seq'), may hold values from -1.75 to 1.75
- w_exp_out: bfloat16 [8, 3072, 768], P('dp', 'seq'), may hold values from -0.625 to 0.625
- exp_out_bias: bfloat16 [8, 768], P('dp', 'seq'), may hold values from -2.5 to 2.5
Outputs:
- block_output: bfloat16 [32, 576, 768], P('dp', 'seq')
- tokens_grad: bfloat16 [32, 576, 768], P('dp', 'seq')
- ln1_gain_grad: float32 [768], P(('dp', 'seq'))
- ln1_shift_grad: float32 [768], P(('dp', 'seq'))
- w_qkv_grad: float32 [768, 2304], P(('dp', 'seq'))
- w_out_grad: float32 [768, 768], P(('dp', 'seq'))
- out_bias_grad: float32 [768], P(('dp', 'seq'))
- ln2_gain_grad: float32 [768], P(('dp', 'seq'))
- ln2_shift_grad: float32 [768], P(('dp', 'seq'))
- w_router_grad: float32 [768, 8], P(('dp', 'seq'))
- w_in_grad: float32 [8, 768, 3072], P('dp', None, 'seq')
- in_bias_grad: float32 [8, 3072], P('dp', 'seq')
- w_exp_out_grad: float32 [8, 3072, 768], P('dp', 'seq')
- exp_out_bias_grad: float32 [8, 768], P('dp', 'seq')
Inputs may be any that keep to these rules, and one draw needn't show every extreme that they name: `pad_mask`: each row is 1 on its first positions and 0 after them; in each aligned group of 4 rows one row is all ones. `priority`: each device's block of 4 rows and 144 positions, read row by row, lists every index r * 144 + p of the block's patches exactly once (r and p the row and position within the block). `expert_ids`: the two ids of a patch differ.
All inputs are finite; a program needn't handle non-finite values.
Results may differ from a plain program's by a relative error of at most 0.017.
Values may be sent and summed in bfloat16 or wider, within the bound.
A program may use at most 192 MiB of HBM per device.

v0:
```python
import jax
import jax.numpy as jnp
from jax import lax
from jax.sharding import PartitionSpec as P

D = 768
HEADS = 12
HEAD = 64


norm_eps = 1e-06


def norm_forward(values, norm_gain, norm_shift):
    average = jnp.mean(values, axis=-1, keepdims=True)
    centred = values - average
    inv_scale = lax.rsqrt(jnp.mean(centred * centred, axis=-1, keepdims=True) + norm_eps)
    normed = centred * inv_scale
    return (
        normed * norm_gain.astype(jnp.float32) + norm_shift.astype(jnp.float32),
        normed,
        inv_scale,
    )


def norm_backward(grad_output, normed, inv_scale, norm_gain):
    scaled = grad_output * norm_gain.astype(jnp.float32)
    grad_input = inv_scale * (
        scaled
        - jnp.mean(scaled, axis=-1, keepdims=True)
        - normed * jnp.mean(scaled * normed, axis=-1, keepdims=True)
    )
    return (
        grad_input,
        jnp.sum(grad_output * normed, axis=(0, 1)),
        jnp.sum(grad_output, axis=(0, 1)),
    )


def gelu_slope(values):
    return (
        0.5 * (1.0 + lax.erf(values * 0.7071067811865476))
        + values * jnp.exp(-0.5 * values * values) * 0.3989422804014327
    )


def pair_slots(order, expert_picks, valid_flags, expert_count, capacity):
    pair_half = order.shape[0]
    token_pairs = jnp.concatenate([order, order])
    which_pick = jnp.concatenate(
        [jnp.zeros((pair_half,), jnp.int32), jnp.ones((pair_half,), jnp.int32)]
    )
    expert_pairs = expert_picks[token_pairs, which_pick]
    valid_pairs = valid_flags[token_pairs]
    matches = (expert_pairs[:, None] == jnp.arange(expert_count, dtype=jnp.int32)[None, :]).astype(
        jnp.int32
    )
    counted = matches * valid_pairs[:, None]
    earlier = jnp.cumsum(counted, axis=0) - counted
    slot_index = jnp.sum(earlier * matches, axis=1)
    kept_flags = valid_pairs * (slot_index < capacity).astype(jnp.int32)
    return (token_pairs, expert_pairs, slot_index, kept_flags)


def shards(
    tokens,
    cotangent,
    pad_mask,
    expert_ids,
    priority,
    ln1_gain,
    ln1_shift,
    w_qkv,
    w_out,
    out_bias,
    ln2_gain,
    ln2_shift,
    w_router,
    w_in,
    in_bias,
    w_exp_out,
    exp_out_bias,
):
    rows_dev, pos_dev = pad_mask.shape
    tok_count = rows_dev * pos_dev
    expert_count = w_router.shape[1]
    local_experts = w_in.shape[0]
    capacity = (21 * tok_count + 10 * expert_count - 1) // (10 * expert_count)
    scale_factor = HEAD ** (-0.5)
    gain_one, shift_one, qkv_weight, out_weight, out_shift, gain_two, shift_two, router_weight = (
        lax.all_gather(ln1_gain, ("dp", "seq"), axis=0, tiled=True),
        lax.all_gather(ln1_shift, ("dp", "seq"), axis=0, tiled=True),
        lax.all_gather(w_qkv, ("dp", "seq"), axis=0, tiled=True),
        lax.all_gather(w_out, ("dp", "seq"), axis=0, tiled=True),
        lax.all_gather(out_bias, ("dp", "seq"), axis=0, tiled=True),
        lax.all_gather(ln2_gain, ("dp", "seq"), axis=0, tiled=True),
        lax.all_gather(ln2_shift, ("dp", "seq"), axis=0, tiled=True),
        lax.all_gather(w_router, ("dp", "seq"), axis=0, tiled=True),
    )
    x_float = tokens.astype(jnp.float32)
    h_one, normed_one, inv_one = norm_forward(x_float, gain_one, shift_one)
    h_one_low = h_one.astype(jnp.bfloat16)
    qkv_low = jnp.einsum(
        "rpd,de->rpe", h_one_low, qkv_weight, preferred_element_type=jnp.float32
    ).astype(jnp.bfloat16)
    queries = qkv_low[:, :, :D].reshape(rows_dev, pos_dev, HEADS, HEAD)
    kv_all, mask_all = (
        lax.all_gather(qkv_low[:, :, D:], "seq", axis=1, tiled=True),
        lax.all_gather(pad_mask.astype(jnp.bfloat16), "seq", axis=1, tiled=True),
    )
    full_len = kv_all.shape[1]
    keys_all = kv_all[:, :, :D].reshape(rows_dev, full_len, HEADS, HEAD)
    values_all = kv_all[:, :, D:].reshape(rows_dev, full_len, HEADS, HEAD)
    key_open = (mask_all > 0)[:, None, None, :]

    def score_block():
        raw_scores = (
            jnp.einsum("rphd,rkhd->rhpk", queries, keys_all, preferred_element_type=jnp.float32)
            * scale_factor
        )
        return jnp.where(key_open, raw_scores, -1e30)

    scores = score_block()
    row_max = jnp.max(scores, axis=-1, keepdims=True)
    exp_scores = jnp.exp(scores - row_max)
    row_total = jnp.sum(exp_scores, axis=-1, keepdims=True)
    log_total = row_max + jnp.log(row_total)
    probs_low = (exp_scores / row_total).astype(jnp.bfloat16)
    attended = (
        jnp.einsum("rhpk,rkhd->rphd", probs_low, values_all, preferred_element_type=jnp.float32)
        .reshape(rows_dev, pos_dev, D)
        .astype(jnp.bfloat16)
    )
    branch = jnp.einsum(
        "rpd,de->rpe", attended, out_weight, preferred_element_type=jnp.float32
    ) + out_shift.astype(jnp.float32)
    resid = x_float + branch
    h_two, normed_two, inv_two = norm_forward(resid, gain_two, shift_two)
    flat_low = h_two.astype(jnp.bfloat16).reshape(tok_count, D)
    logits = jnp.dot(flat_low, router_weight, preferred_element_type=jnp.float32)
    router_probs = jax.nn.softmax(logits, axis=-1)
    token_pairs, expert_pairs, slot_index, kept_flags = pair_slots(
        priority.reshape(-1),
        expert_ids.reshape(tok_count, 2),
        pad_mask.reshape(-1),
        expert_count,
        capacity,
    )
    dummy_row = expert_count * capacity
    destination = jnp.where(kept_flags > 0, expert_pairs * capacity + slot_index, dummy_row)
    kept_float = kept_flags.astype(jnp.float32)
    gate_pairs = router_probs[token_pairs, expert_pairs] * kept_float
    send_rows = (
        jnp.zeros((dummy_row + 1, D), jnp.bfloat16)
        .at[destination]
        .set(flat_low[token_pairs])[:-1]
        .reshape(expert_count, capacity, D)
    )
    received = lax.all_to_all(send_rows, "dp", split_axis=0, concat_axis=1, tiled=True)
    seq_index = lax.axis_index("seq")
    bias_cols = exp_out_bias.shape[1]
    rows_all = lax.all_gather(received, "seq", axis=1, tiled=True)
    pre_act = (
        jnp.einsum("erd,edf->erf", rows_all, w_in, preferred_element_type=jnp.float32)
        + in_bias.astype(jnp.float32)[:, None, :]
    )
    act_low = jax.nn.gelu(pre_act, approximate=False).astype(jnp.bfloat16)
    partial_out = jnp.einsum("erf,efd->erd", act_low, w_exp_out, preferred_element_type=jnp.float32)
    bias_full = lax.dynamic_update_slice_in_dim(
        jnp.zeros((local_experts, D), jnp.float32),
        exp_out_bias.astype(jnp.float32),
        seq_index * bias_cols,
        1,
    )
    partial_out = partial_out + bias_full[:, None, :]
    expert_out = lax.psum_scatter(
        partial_out.astype(jnp.bfloat16), "seq", scatter_dimension=1, tiled=True
    )
    returned_buf = lax.all_to_all(expert_out, "dp", split_axis=1, concat_axis=0, tiled=True)
    returned = jnp.concatenate(
        [returned_buf.reshape(-1, D), jnp.zeros((1, D), jnp.bfloat16)], axis=0
    )[destination].astype(jnp.float32)
    mixture = (
        jnp.zeros((tok_count, D), jnp.float32).at[token_pairs].add(gate_pairs[:, None] * returned)
    )
    block_output = (resid + mixture.reshape(rows_dev, pos_dev, D)).astype(jnp.bfloat16)
    grad_y = cotangent.astype(jnp.float32)
    grad_pairs = grad_y.reshape(tok_count, D)[token_pairs]
    grad_gates = jnp.sum(grad_pairs * returned, axis=-1) * kept_float
    grad_ret = (gate_pairs[:, None] * grad_pairs).astype(jnp.bfloat16)
    grad_send = (
        jnp.zeros((dummy_row + 1, D), jnp.bfloat16)
        .at[destination]
        .set(grad_ret)[:-1]
        .reshape(expert_count, capacity, D)
    )
    grad_recv = lax.all_to_all(grad_send, "dp", split_axis=0, concat_axis=1, tiled=True)
    grad_all = lax.all_gather(grad_recv, "seq", axis=1, tiled=True)
    pre_again = (
        jnp.einsum("erd,edf->erf", rows_all, w_in, preferred_element_type=jnp.float32)
        + in_bias.astype(jnp.float32)[:, None, :]
    )
    act_again = jax.nn.gelu(pre_again, approximate=False).astype(jnp.bfloat16)
    grad_act = jnp.einsum("erd,efd->erf", grad_all, w_exp_out, preferred_element_type=jnp.float32)
    grad_pre = (grad_act * gelu_slope(pre_again)).astype(jnp.bfloat16)
    w_exp_out_grad = jnp.einsum(
        "erf,erd->efd", act_again, grad_all, preferred_element_type=jnp.float32
    )
    bias_sums = jnp.sum(grad_all, axis=1, dtype=jnp.float32)
    exp_out_bias_grad = lax.dynamic_slice_in_dim(bias_sums, seq_index * bias_cols, bias_cols, 1)
    w_in_grad = jnp.einsum("erd,erf->edf", rows_all, grad_pre, preferred_element_type=jnp.float32)
    in_bias_grad = jnp.sum(grad_pre, axis=1, dtype=jnp.float32)
    grad_rows_part = jnp.einsum("erf,edf->erd", grad_pre, w_in, preferred_element_type=jnp.float32)
    grad_back = lax.psum_scatter(
        grad_rows_part.astype(jnp.bfloat16), "seq", scatter_dimension=1, tiled=True
    )
    grad_buf = lax.all_to_all(grad_back, "dp", split_axis=1, concat_axis=0, tiled=True)
    grad_rows_back = jnp.concatenate(
        [grad_buf.reshape(-1, D), jnp.zeros((1, D), jnp.bfloat16)], axis=0
    )[destination].astype(jnp.float32)
    grad_h2_experts = jnp.zeros((tok_count, D), jnp.float32).at[token_pairs].add(grad_rows_back)
    grad_probs = (
        jnp.zeros((tok_count, expert_count), jnp.float32)
        .at[token_pairs, expert_pairs]
        .add(grad_gates)
    )
    grad_logits = (
        router_probs * (grad_probs - jnp.sum(router_probs * grad_probs, axis=-1, keepdims=True))
    ).astype(jnp.bfloat16)
    router_grad = jnp.einsum("td,te->de", flat_low, grad_logits, preferred_element_type=jnp.float32)
    grad_h2 = grad_h2_experts + jnp.einsum(
        "te,de->td", grad_logits, router_weight, preferred_element_type=jnp.float32
    )
    grad_resid_norm, gain_two_grad, shift_two_grad = norm_backward(
        grad_h2.reshape(rows_dev, pos_dev, D), normed_two, inv_two, gain_two
    )
    grad_resid = grad_y + grad_resid_norm
    grad_branch = grad_resid.astype(jnp.bfloat16)
    out_weight_grad = jnp.einsum(
        "rpd,rpe->de", attended, grad_branch, preferred_element_type=jnp.float32
    )
    out_shift_grad = jnp.sum(grad_branch, axis=(0, 1), dtype=jnp.float32)
    grad_attended = jnp.einsum(
        "rpe,de->rpd", grad_branch, out_weight, preferred_element_type=jnp.float32
    ).astype(jnp.bfloat16)
    grad_att_heads = grad_attended.reshape(rows_dev, pos_dev, HEADS, HEAD)
    scores_again = score_block()
    probs_again = jnp.exp(scores_again - log_total)
    probs_again_low = probs_again.astype(jnp.bfloat16)
    grad_probs_att = jnp.einsum(
        "rphd,rkhd->rhpk", grad_att_heads, values_all, preferred_element_type=jnp.float32
    )
    row_delta = jnp.sum(probs_again * grad_probs_att, axis=-1, keepdims=True)
    grad_scores = (probs_again * (grad_probs_att - row_delta)).astype(jnp.bfloat16)
    grad_queries = (
        jnp.einsum("rhpk,rkhd->rphd", grad_scores, keys_all, preferred_element_type=jnp.float32)
        * scale_factor
    ).reshape(rows_dev, pos_dev, D)
    grad_keys = (
        jnp.einsum("rhpk,rphd->rkhd", grad_scores, queries, preferred_element_type=jnp.float32)
        * scale_factor
    ).reshape(rows_dev, full_len, D)
    grad_values = jnp.einsum(
        "rhpk,rphd->rkhd", probs_again_low, grad_att_heads, preferred_element_type=jnp.float32
    ).reshape(rows_dev, full_len, D)
    grad_kv = lax.psum_scatter(
        jnp.concatenate([grad_keys, grad_values], axis=-1).astype(jnp.bfloat16),
        "seq",
        scatter_dimension=1,
        tiled=True,
    )
    grad_qkv = jnp.concatenate([grad_queries.astype(jnp.bfloat16), grad_kv], axis=-1)
    qkv_weight_grad = jnp.einsum(
        "rpd,rpe->de", h_one_low, grad_qkv, preferred_element_type=jnp.float32
    )
    grad_h1 = jnp.einsum("rpe,de->rpd", grad_qkv, qkv_weight, preferred_element_type=jnp.float32)
    grad_x_norm, gain_one_grad, shift_one_grad = norm_backward(
        grad_h1, normed_one, inv_one, gain_one
    )
    tokens_grad = (grad_resid + grad_x_norm).astype(jnp.bfloat16)
    dense_parts = (
        lax.psum_scatter(gain_one_grad, ("dp", "seq"), scatter_dimension=0, tiled=True),
        lax.psum_scatter(shift_one_grad, ("dp", "seq"), scatter_dimension=0, tiled=True),
        lax.psum_scatter(qkv_weight_grad, ("dp", "seq"), scatter_dimension=0, tiled=True),
        lax.psum_scatter(out_weight_grad, ("dp", "seq"), scatter_dimension=0, tiled=True),
        lax.psum_scatter(out_shift_grad, ("dp", "seq"), scatter_dimension=0, tiled=True),
        lax.psum_scatter(gain_two_grad, ("dp", "seq"), scatter_dimension=0, tiled=True),
        lax.psum_scatter(shift_two_grad, ("dp", "seq"), scatter_dimension=0, tiled=True),
        lax.psum_scatter(router_grad, ("dp", "seq"), scatter_dimension=0, tiled=True),
    )
    return (
        block_output,
        tokens_grad,
        dense_parts[0],
        dense_parts[1],
        dense_parts[2],
        dense_parts[3],
        dense_parts[4],
        dense_parts[5],
        dense_parts[6],
        dense_parts[7],
        w_in_grad,
        in_bias_grad,
        w_exp_out_grad,
        exp_out_bias_grad,
    )


def solution(mesh):
    return jax.shard_map(
        shards,
        mesh=mesh,
        in_specs=(
            P("dp", "seq", None),
            P("dp", "seq", None),
            P("dp", "seq"),
            P("dp", "seq", None),
            P("dp", "seq"),
            P(("dp", "seq")),
            P(("dp", "seq")),
            P(("dp", "seq"), None),
            P(("dp", "seq"), None),
            P(("dp", "seq")),
            P(("dp", "seq")),
            P(("dp", "seq")),
            P(("dp", "seq"), None),
            P("dp", None, "seq"),
            P("dp", "seq"),
            P("dp", "seq", None),
            P("dp", "seq"),
        ),
        out_specs=(
            P("dp", "seq", None),
            P("dp", "seq", None),
            P(("dp", "seq")),
            P(("dp", "seq")),
            P(("dp", "seq"), None),
            P(("dp", "seq"), None),
            P(("dp", "seq")),
            P(("dp", "seq")),
            P(("dp", "seq")),
            P(("dp", "seq"), None),
            P("dp", None, "seq"),
            P("dp", "seq"),
            P("dp", "seq", None),
            P("dp", "seq"),
        ),
        check_vma=False,
    )
```

profile of v0, /device:TPU:0, one launch (start us, length us, event | category | flops | bytes accessed | tf_op | source)
XLA Modules:
  0.0 1289.1 jit_solution(2935522465288049803)
XLA Ops:
  12.2 42.2 %all-reduce.14 = (bf16[768]{0:T(1024)(128)(2,1)S(1)}, bf16[768]{0:T(1024)(128)(2,1)S(1)}, bf16[768]{0:T(1024)(128)(2,1)S(1)}, bf16[768]{0:T(1024)(128)(2,1)S(1)}, bf16[768]{0:T(1024)(128)(2,1)S(1)}) all-reduce(bf16[768]{0:T(1024)(128)(2,1)S(1)} %dynamic-update-slice.1, ...), channel_id=1, replica_groups=mesh['dp'=8,'seq'=4] {'dp','seq'}, use_global_device_ids=true, to_apply=%add.3 | all-reduce | flops 3840 | bytes 15360
  57.7 16.1 %all-gather.8.cloned.1.call-done = bf16[768,2304]{1,0:T(8,128)(2,1)} async-done(((bf16[24,2304]{1,0:T(8,128)(2,1)}), bf16[768,2304]{1,0:T(8,128)(2,1)}) %all-gather.8.cloned.1.call-update) | async-done | bytes 3538960 | tf_op jit(solution)/shard_map/all_gather | solution.py:93
  111.2 20.1 %all-gather.10.cloned.1.call-done = bf16[4,576,1536]{2,1,0:T(8,128)(2,1)} async-done(((bf16[4,144,1536]{2,1,0:T(8,128)(2,1)}), bf16[4,576,1536]{2,1,0:T(8,128)(2,1)}) %all-gather.10.cloned.1.call-update) | async-done | bytes 7077904 | tf_op jit(solution)/shard_map/all_gather | solution.py:108
  173.3 15.0 %all-gather.12.cloned.1.call-done = bf16[768,768]{1,0:T(8,128)(2,1)} async-done(((bf16[24,768]{1,0:T(8,128)(2,1)}), bf16[768,768]{1,0:T(8,128)(2,1)}) %all-gather.12.cloned.1.call-update) | async-done | bytes 1179664 | tf_op jit(solution)/shard_map/all_gather | solution.py:94
  192.8 19.2 %scatter_custom_fusion = bf16[1217,768]{1,0:T(8,128)(2,1)} fusion(s32[1152]{0:T(1024)S(1)} %fusion.91, bf16[576,768]{1,0:T(8,128)(2,1)S(1)} %bitcast.181, s32[2048]{0:T(1024)S(1)} %pad_clamp_fusion.1, bf16[]{:T(256)} %constant.51.clone.1), kind=kCustom, calls=%fused_computation.101 | custom fusion | bytes 1869314 | tf_op jit(solution)/shard_map/scatter | solution.py:156
  213.5 48.8 %all_to_all.42 = bf16[8,152,768]{2,1,0:T(8,128)(2,1)} all-to-all(bf16[8,152,768]{2,1,0:T(8,128)(2,1)S(1)} %bitcast.184), channel_id=1, replica_groups=mesh['dp'=8,'seq'=4] {'dp'}, dimensions={0} | all-to-all | bytes 3735552 | tf_op jit(solution)/shard_map/all_to_all | solution.py:159
  263.1 49.8 %all-gather.14.cloned.1.call-done = bf16[1,4864,768]{2,1,0:T(8,128)(2,1)} async-done(((bf16[1,1216,768]{2,1,0:T(8,128)(2,1)}), bf16[1,4864,768]{2,1,0:T(8,128)(2,1)}) %all-gather.14.cloned.1.call-update) | async-done | bytes 7471120 | tf_op jit(solution)/shard_map/all_gather | solution.py:162
  312.9 39.3 %fusion.3 = (bf16[4864,768]{1,0:T(8,128)(2,1)S(1)}, f32[4864,768]{1,0:T(8,128)}) fusion(f32[768]{0:T(1024)S(1)} %convert_reduce_fusion.4, bf16[1,768,768]{2,1,0:T(8,128)(2,1)S(1)} %copy-done, bf16[1,4864,768]{2,1,0:T(8,128)(2,1)} %all-gather.14.cloned.1.call-done), kind=kOutput, calls=%fused_computation.23 | convolution fusion | flops 5984354304 | bytes 31067136 | tf_op jit(solution)/shard_map/erd,edf->erf/dot_general | solution.py:164
  363.4 66.5 %reduce-scatter.7.cloned.1.call-done = bf16[1,1216,768]{2,1,0:T(8,128)(2,1)} async-done(((bf16[1,4864,768]{2,1,0:T(8,128)(2,1)}), bf16[1,1216,768]{2,1,0:T(8,128)(2,1)}) %reduce-scatter.7.cloned.1.call-update) | async-done | bytes 1867792 | tf_op jit(solution)/shard_map/reduce_scatter | solution.py:176
  460.7 66.2 %all-gather.1 = bf16[32,24,8]{1,2,0:T(8,128)(2,1)S(1)} all-gather(bf16[1,24,8]{1,2,0:T(8,128)(2,1)S(1)} %bitcast.205), channel_id=1, replica_groups=mesh['dp'=8,'seq'=4] {'dp','seq'}, dimensions={0}, use_global_device_ids=true | all-gather | bytes 12672 | tf_op jit(solution)/shard_map/all_gather | solution.py:98
  566.4 14.0 %scatter_custom_fusion.2 = bf16[1217,768]{1,0:T(8,128)(2,1)S(1)} fusion(s32[1152]{0:T(1024)S(1)} %fusion.91, f32[1152,768]{1,0:T(8,128)} %gather_fusion.4, f32[1152]{0:T(1024)S(1)} %convert_multiply_fusion.4, bf16[]{:T(256)} %constant.51.clone.1), kind=kCustom, calls=%fused_computation.100 | custom fusion | flops 1769472 | bytes 5416450 | tf_op jit(solution)/shard_map/scatter | solution.py:194
  580.6 50.0 %all_to_all.43 = bf16[8,152,768]{2,1,0:T(8,128)(2,1)} all-to-all(bf16[8,152,768]{2,1,0:T(8,128)(2,1)S(1)} %bitcast.187), channel_id=1, replica_groups=mesh['dp'=8,'seq'=4] {'dp'}, dimensions={0} | all-to-all | bytes 3735552 | tf_op jit(solution)/shard_map/all_to_all | solution.py:197
  630.6 50.5 %all-gather.16.cloned.1.call-done = bf16[1,4864,768]{2,1,0:T(8,128)(2,1)} async-done(((bf16[1,1216,768]{2,1,0:T(8,128)(2,1)}), bf16[1,4864,768]{2,1,0:T(8,128)(2,1)}) %all-gather.16.cloned.1.call-update) | async-done | bytes 7471120 | tf_op jit(solution)/shard_map/all_gather | solution.py:198
  681.2 13.2 %convert_reduce_fusion.1 = (f32[768]{0:T(1024)S(1)}, bf16[4864,768]{1,0:T(8,128)(2,1)S(1)}) fusion(f32[4864,768]{1,0:T(8,128)} %get-tuple-element.50, f32[768]{0:T(1024)S(1)} %convert_reduce_fusion.4, bf16[1,768,768]{2,1,0:T(8,128)(2,1)S(1)} %copy-done.60, bf16[1,4864,768]{2,1,0:T(8,128)(2,1)} %all-gather.16.cloned.1.call-done), kind=kOutput, calls=%fused_computation.31 | convolution fusion | flops 5786369024 | bytes 31070208 | tf_op jit(solution)/shard_map/erd,efd->erf/dot_general | solution.py:204
  705.4 66.5 %reduce-scatter.9.cloned.1.call-done = bf16[1,1216,768]{2,1,0:T(8,128)(2,1)} async-done(((bf16[1,4864,768]{2,1,0:T(8,128)(2,1)}), bf16[1,1216,768]{2,1,0:T(8,128)(2,1)}) %reduce-scatter.9.cloned.1.call-update) | async-done | bytes 1867792 | tf_op jit(solution)/shard_map/reduce_scatter | solution.py:214
  781.4 13.2 %reduce.22 = bf16[1216,768]{1,0:T(8,128)(2,1)} reduce(bf16[1216,1,768]{2,1,0:T(2,128)(2,1)} %bitcast.176, bf16[]{:T(256)} %broadcast.585), dimensions={1}, to_apply=%bitcast.163.reduce_sub_computation | reduce | bytes 3735554
  806.1 13.5 %scatter_custom_fusion.1 = f32[576,768]{1,0:T(8,128)} fusion(s32[1152]{0:T(1024)} %copy-done.48, bf16[1152,768]{1,0:T(8,128)(2,1)S(1)} %copy-done.6, f32[1152]{0:T(1024)S(1)} %convert_multiply_fusion.4, f32[]{:T(128)} %constant.48.clone.1), kind=kCustom, calls=%fused_computation.69 | custom fusion | flops 2654208 | bytes 3544064 | tf_op jit(solution)/shard_map/scatter-add | solution.py:184
  821.2 28.2 %all-to-all-done.3 = bf16[8,2,58368]{2,1,0:T(2,128)(2,1)} async-done(((bf16[8,2,58368]{2,1,0:T(2,128)(2,1)}), bf16[8,2,58368]{2,1,0:T(2,128)(2,1)}, u32[]{:S(2)}, u32[]{:S(2)}) %all-to-all-start.3) | async-done | bytes 1867808 | tf_op jit(solution)/shard_map/all_to_all | solution.py:217
  859.7 28.2 %scatter_custom_fusion.3 = f32[576,768]{1,0:T(8,128)} fusion(f32[576,768]{1,0:T(8,128)} %fusion.106, s32[1152]{0:T(1024)} %copy-done.48, bf16[1217,768]{1,0:T(8,128)(2,1)} %concatenate.49, s32[2048]{0:T(1024)S(1)} %pad_clamp_fusion), kind=kCustom, calls=%fused_computation.74 | custom fusion | flops 1769472 | bytes 3657728 | tf_op jit(solution)/shard_map/scatter-add | solution.py:221
  910.4 16.2 %multiply_reduce_fusion = (f32[4,12,144]{2,1,0:T(8,128)S(1)}, f32[4,12,144,576]{3,2,1,0:T(8,128)}) fusion(f32[4,12,144]{2,1,0:T(8,128)S(1)} %log_add_fusion, f32[4,12,144,576]{3,2,1,0:T(8,128)} %copy-done.1, pred[4,576]{1,0:T(4,128)(4,1)S(1)} %bitcast.199, bf16[4,144,12,64]{1,3,2,0:T(8,128)(2,1)S(1)} %bitcast.192, bf16[4,576,12,64]{1,3,2,0:T(8,128)(2,1)S(1)} %bitcast.173), kind=kOutput, calls=%fused_computation.15 | convolution fusion | flops 529507584 | bytes 36331776 | tf_op jit(solution)/shard_map/rphd,rkhd->rhpk/dot_general | solution.py:250
  979.8 72.2 %reduce-scatter.11.cloned.1.call-done = bf16[4,144,1536]{2,1,0:T(8,128)(2,1)} async-done(((bf16[4,576,1536]{2,1,0:T(8,128)(2,1)}), bf16[4,144,1536]{2,1,0:T(8,128)(2,1)}) %reduce-scatter.11.cloned.1.call-update) | async-done | bytes 1769488 | tf_op jit(solution)/shard_map/reduce_scatter | solution.py:266
  1088.9 40.4 %all-reduce.13 = (f32[768]{0:T(1024)S(1)}, f32[768]{0:T(1024)S(1)}, f32[768]{0:T(1024)S(1)}, f32[768]{0:T(1024)S(1)}, f32[768]{0:T(1024)S(1)}, /*index=5*/f32[768,8]{0,1:T(8,128)S(1)}) all-reduce(f32[768]{0:T(1024)S(1)} %get-tuple-element.16, f32[768]{0:T(1024)S(1)} %get-tuple-element.21, ...), channel_id=5, replica_groups=mesh['dp'=8,'seq'=4] {'dp','seq'}, use_global_device_ids=true, to_apply=%region_27.28.clone | all-reduce | flops 9984 | bytes 79872
  1136.5 21.4 %reduce-scatter.15.cloned.1.call-done = f32[24,768]{1,0:T(8,128)} async-done(((f32[768,768]{1,0:T(8,128)}), f32[24,768]{1,0:T(8,128)}) %reduce-scatter.15.cloned.1.call-update) | async-done | bytes 73744 | tf_op jit(solution)/shard_map/reduce_scatter | solution.py:285
  1157.9 124.1 %reduce-scatter.13.cloned.1.call-done = f32[24,2304]{1,0:T(8,128)} async-done(((f32[768,2304]{1,0:T(8,128)}), f32[24,2304]{1,0:T(8,128)}) %reduce-scatter.13.cloned.1.call-update) | async-done | bytes 221200 | tf_op jit(solution)/shard_map/reduce_scatter | solution.py:284
  (291 shorter events, 338.9 us)
Async XLA Ops:
  7.2 305.8 %copy-start = (bf16[1,768,768]{2,1,0:T(8,128)(2,1)S(1)}, bf16[1,768,768]{2,1,0:T(8,128)(2,1)}, u32[]{:S(2)}) copy-start(bf16[1,768,768]{2,1,0:T(8,128)(2,1)} %param.30) | copy-start | bytes 3538948
  7.2 66.6 %all-gather.8.cloned.1.call-start = ((), (), s32[]{:S(2)}) async-start(), calls=%async_computation.9 | async-start | bytes 3649536 | tf_op jit(solution)/shard_map/all_gather | solution.py:93
  7.9 123.3 %all-gather.10.cloned.1.call-start = ((), (), s32[]{:S(2)}) async-start(), calls=%async_computation.10 | async-start | bytes 8847360 | tf_op jit(solution)/shard_map/all_gather | solution.py:108
  81.4 106.9 %all-gather.12.cloned.1.call-start = ((), (), s32[]{:S(2)}) async-start(), calls=%async_computation.11 | async-start | bytes 1216512 | tf_op jit(solution)/shard_map/all_gather | solution.py:94
  82.1 230.8 %all-gather.14.cloned.1.call-start = ((), (), s32[]{:S(2)}) async-start(), calls=%async_computation.12 | async-start | bytes 9338880 | tf_op jit(solution)/shard_map/all_gather | solution.py:162
  82.4 109.2 %copy-start.39 = (f32[768]{0:T(1024)}, f32[768]{0:T(1024)S(1)}, u32[]{:S(2)}) copy-start(f32[768]{0:T(1024)S(1)} %convert_element_type.141) | copy-start | bytes 9220
  87.9 75.2 %copy-start.25 = (pred[576,4]{0,1:T(4,128)(4,1)}, pred[576,4]{0,1:T(4,128)(4,1)S(1)}, u32[]{:S(2)}) copy-start(pred[576,4]{0,1:T(4,128)(4,1)S(1)} %reshape.593) | copy-start | bytes 6916
  192.7 69.6 %copy-start.13 = (bf16[4,144,768]{2,1,0:T(8,128)(2,1)}, bf16[4,144,768]{2,1,0:T(8,128)(2,1)S(1)}, u32[]{:S(2)}) copy-start(bf16[4,144,768]{2,1,0:T(8,128)(2,1)S(1)} %add_convert_fusion.2) | copy-start | bytes 2654212
  262.3 167.6 %reduce-scatter.7.cloned.1.call-start = ((), (), s32[]{:S(2)}) async-start(), calls=%async_computation.13 | async-start | bytes 9338880 | tf_op jit(solution)/shard_map/reduce_scatter | solution.py:176
  263.1 92.1 %copy-start.59 = (bf16[1,768,768]{2,1,0:T(8,128)(2,1)S(1)}, bf16[1,768,768]{2,1,0:T(8,128)(2,1)}, u32[]{:S(2)}) copy-start(bf16[1,768,768]{2,1,0:T(8,128)(2,1)} %param.32) | copy-start | bytes 3538948
  455.1 80.1 %all-to-all-start.1 = ((bf16[8,2,58368]{2,1,0:T(2,128)(2,1)}), bf16[8,2,58368]{2,1,0:T(2,128)(2,1)}, u32[]{:S(2)}, u32[]{:S(2)}) async-start(bf16[8,2,58368]{2,1,0:T(2,128)(2,1)} %reshape.628), calls=%async_computation.2 | async-start | bytes 3735552 | tf_op jit(solution)/shard_map/all_to_all | solution.py:179
  460.6 220.6 %all-gather.16.cloned.1.call-start = ((), (), s32[]{:S(2)}) async-start(), calls=%async_computation.14 | async-start | bytes 9338880 | tf_op jit(solution)/shard_map/all_gather | solution.py:198
  580.5 100.6 %copy-start.60 = (bf16[1,768,768]{2,1,0:T(8,128)(2,1)S(1)}, bf16[1,768,768]{2,1,0:T(8,128)(2,1)}, u32[]{:S(2)}) copy-start(bf16[1,768,768]{2,1,0:T(8,128)(2,1)} %param.32) | copy-start | bytes 3538948
  630.6 141.3 %reduce-scatter.9.cloned.1.call-start = ((), (), s32[]{:S(2)}) async-start(), calls=%async_computation.15 | async-start | bytes 9338880 | tf_op jit(solution)/shard_map/reduce_scatter | solution.py:214
  800.5 48.9 %all-to-all-start.3 = ((bf16[8,2,58368]{2,1,0:T(2,128)(2,1)}), bf16[8,2,58368]{2,1,0:T(2,128)(2,1)}, u32[]{:S(2)}, u32[]{:S(2)}) async-start(bf16[8,2,58368]{2,1,0:T(2,128)(2,1)} %reshape.630), calls=%async_computation.5 | async-start | bytes 3735552 | tf_op jit(solution)/shard_map/all_to_all | solution.py:217
  806.0 246.0 %reduce-scatter.11.cloned.1.call-start = ((), (), s32[]{:S(2)}) async-start(), calls=%async_computation.16 | async-start | bytes 8847360 | tf_op jit(solution)/shard_map/reduce_scatter | solution.py:266
  962.8 195.1 %reduce-scatter.15.cloned.1.call-start = ((), (), s32[]{:S(2)}) async-start(), calls=%async_computation.18 | async-start | bytes 2433024 | tf_op jit(solution)/shard_map/reduce_scatter | solution.py:285
  968.3 83.7 %copy-start.12 = (bf16[4,144,768]{2,1,0:T(8,128)(2,1)S(1)}, bf16[4,144,768]{2,1,0:T(8,128)(2,1)}, u32[]{:S(2)}) copy-start(bf16[4,144,768]{2,1,0:T(8,128)(2,1)} %param.17) | copy-start | bytes 2654212
  968.3 83.7 %copy-start.24 = (f32[4,144]{1,0:T(4,128)S(1)}, f32[4,144]{1,0:T(4,128)}, u32[]{:S(2)}) copy-start(f32[4,144]{1,0:T(4,128)} %copy-done.23) | copy-start | bytes 6916
  968.3 83.7 %copy-start.32 = (f32[768]{0:T(1024)S(1)}, f32[768]{0:T(1024)}, u32[]{:S(2)}) copy-start(f32[768]{0:T(1024)} %copy-done.31) | copy-start | bytes 9220
  968.3 83.7 %copy-start.34 = (f32[4,144]{1,0:T(4,128)S(1)}, f32[4,144]{1,0:T(4,128)}, u32[]{:S(2)}) copy-start(f32[4,144]{1,0:T(4,128)} %copy-done.33) | copy-start | bytes 6916
  968.3 83.7 %copy-start.36 = (f32[768]{0:T(1024)S(1)}, f32[768]{0:T(1024)}, u32[]{:S(2)}) copy-start(f32[768]{0:T(1024)} %copy-done.35) | copy-start | bytes 9220
  968.3 313.7 %reduce-scatter.13.cloned.1.call-start = ((), (), s32[]{:S(2)}) async-start(), calls=%async_computation.17 | async-start | bytes 7299072 | tf_op jit(solution)/shard_map/reduce_scatter | solution.py:284
  979.8 78.9 %copy-start.17 = (bf16[4,144,768]{2,1,0:T(8,128)(2,1)}, bf16[4,144,768]{2,1,0:T(8,128)(2,1)S(1)}, u32[]{:S(2)}) copy-start(bf16[4,144,768]{2,1,0:T(8,128)(2,1)S(1)} %copy.109) | copy-start | bytes 2654212
  (57 other events, 700.2 us)
Sparse Core Ops, SparseCore 0:
  10.9 62.8 all-gather.7
  81.5 49.6 all-gather.9
  134.1 54.0 all-gather.11
  262.5 50.4 all-gather.13
  363.6 66.3 reduce-scatter.6
  630.7 50.4 all-gather.15
  705.5 66.3 reduce-scatter.8
  962.9 89.0 reduce-scatter.10
  1058.7 99.1 reduce-scatter.14
  1164.0 118.0 reduce-scatter.12
where the time goes:
time: 1290 us
  waiting for transfers between devices  532 us (41%)
  blocking collectives  253 us (20%)
  matrix products  171 us (13%)
  local copies, waits for them, and re-layouts  166 us (13%)
  other arithmetic  141 us (11%)
  between operations  15.4 us (1%)
    reduce_scatter x1, waiting for transfers between devices, shards(): lax.psum_scatter(qkv_weight_grad, ('dp', 'seq'), scatter_dimension=0, til...  124 us
    unnamed x2, blocking collectives  82.6 us
    reduce_scatter x1, waiting for transfers between devices, shards(): lax.psum_scatter(jnp.concatenate([grad_keys, grad_values], axis=-1).astyp...  72.2 us
    reduce_scatter x1, waiting for transfers between devices, shards(): lax.psum_scatter(partial_out.astype(jnp.bfloat16), 'seq', scatter_dimensi...  66.5 us
    reduce_scatter x1, waiting for transfers between devices, shards(): lax.psum_scatter(grad_rows_part.astype(jnp.bfloat16), 'seq', scatter_dime...  66.5 us
    all_gather x1, blocking collectives, shards(): lax.all_gather(w_router, ('dp', 'seq'), axis=0, tiled=True)  66.2 us
    unnamed x162, local copies, waits for them, and re-layouts  51.4 us
    all_gather x1, waiting for transfers between devices, shards(): grad_all = lax.all_gather(grad_recv, 'seq', axis=1, tiled=True)  50.5 us
  transfers between devices with their start and end apart: 12, of which 11 were waited for; matrix products, arithmetic and copies ran while one was open for 12% of the time, Pallas kernels for 0%

commit v1 on v0

--- a/solution.py
+++ b/solution.py
@@ -44,25 +44,37 @@
     )
 
 
+def slot_ranks(order, picks, valid, experts, capacity):
+    count = order.shape[0]
+    index = jnp.arange(count, dtype=jnp.int32)
+    rank = jnp.sum(jnp.where(order[:, None] == index[None, :], index[:, None], 0), axis=0)
+    earlier = (rank[None, :] < rank[:, None]).astype(jnp.bfloat16)
+    chosen = picks[:, :, None] == jnp.arange(experts, dtype=jnp.int32)
+    counted = chosen.astype(jnp.float32) * valid.astype(jnp.float32)[:, None, None]
+    before = jnp.dot(
+        earlier,
+        counted.reshape(count, 2 * experts).astype(jnp.bfloat16),
+        preferred_element_type=jnp.float32,
+    ).reshape(count, 2, experts)
+    firsts = jnp.sum(counted[:, 0], axis=0)
+    before = before + jnp.stack([jnp.zeros_like(firsts), firsts])[None]
+    slot = jnp.sum(jnp.where(chosen, before, 0.0), axis=2).astype(jnp.int32)
+    kept = (valid[:, None] > 0) & (slot < capacity)
+    return kept, slot
+
+
 def pair_slots(order, expert_picks, valid_flags, expert_count, capacity):
-    pair_half = order.shape[0]
-    token_pairs = jnp.concatenate([order, order])
-    which_pick = jnp.concatenate(
-        [jnp.zeros((pair_half,), jnp.int32), jnp.ones((pair_half,), jnp.int32)]
-    )
-    expert_pairs = expert_picks[token_pairs, which_pick]
-    valid_pairs = valid_flags[token_pairs]
-    matches = (expert_pairs[:, None] == jnp.arange(expert_count, dtype=jnp.int32)[None, :]).astype(
-        jnp.int32
-    )
-    counted = matches * valid_pairs[:, None]
-    earlier = jnp.cumsum(counted, axis=0) - counted
-    slot_index = jnp.sum(earlier * matches, axis=1)
-    kept_flags = valid_pairs * (slot_index < capacity).astype(jnp.int32)
-    return (token_pairs, expert_pairs, slot_index, kept_flags)
-
-
-def shards(
+    kept, slot = slot_ranks(order, expert_picks, valid_flags, expert_count, capacity)
+    tokens = jnp.arange(order.shape[0], dtype=jnp.int32)
+    return (
+        jnp.concatenate([tokens, tokens]),
+        expert_picks.T.reshape(-1),
+        slot.T.reshape(-1),
+        kept.T.reshape(-1).astype(jnp.int32),
+    )
+
+
+def shards_general(
     tokens,
     cotangent,
     pad_mask,
@@ -306,6 +318,215 @@
     )
 
 
+def mm(a, b, contract, low=False):
+    out = lax.dot_general(a, b, (contract, ((), ())), preferred_element_type=jnp.float32)
+    return out.astype(jnp.bfloat16) if low else out
+
+
+def norm_stats(values):
+    average = jnp.mean(values, axis=-1, keepdims=True)
+    centred = values - average
+    inv = lax.rsqrt(jnp.mean(centred * centred, axis=-1, keepdims=True) + norm_eps)
+    return centred * inv, inv
+
+
+def norm_grad(grad_output, normed, inv, gain):
+    scaled = grad_output * gain
+    return inv * (
+        scaled
+        - jnp.mean(scaled, axis=-1, keepdims=True)
+        - normed * jnp.mean(scaled * normed, axis=-1, keepdims=True)
+    )
+
+
+def to_row(block):
+    return lax.all_to_all(block, "seq", split_axis=0, concat_axis=1, tiled=True)[0]
+
+
+def to_block(row, rows_dev):
+    split = row.reshape(rows_dev, row.shape[0] // rows_dev, row.shape[1])
+    return lax.all_to_all(split, "seq", split_axis=0, concat_axis=0, tiled=True)
+
+
+def shards_rows(
+    tokens,
+    cotangent,
+    pad_mask,
+    expert_ids,
+    priority,
+    ln1_gain,
+    ln1_shift,
+    w_qkv,
+    w_out,
+    out_bias,
+    ln2_gain,
+    ln2_shift,
+    w_router,
+    w_in,
+    in_bias,
+    w_exp_out,
+    exp_out_bias,
+):
+    both = ("dp", "seq")
+    rows_dev, pos_dev = pad_mask.shape
+    tok = rows_dev * pos_dev
+    experts = w_router.shape[1]
+    cap = (21 * tok + 10 * experts - 1) // (10 * experts)
+    n_seq = lax.axis_size("seq")
+    bf, f32 = jnp.bfloat16, jnp.float32
+    vectors = jnp.stack([ln1_gain, ln1_shift, out_bias, ln2_gain, ln2_shift], axis=1)
+    pad = jnp.zeros((vectors.shape[0], 128 - 5 - experts), bf)
+    packed = lax.all_gather(
+        jnp.concatenate([w_qkv, w_out, vectors, w_router, pad], axis=1), both, axis=0, tiled=True
+    )
+    qkv_weight, out_weight = packed[:, : 3 * D], packed[:, 3 * D : 4 * D]
+    vectors = packed[:, 4 * D : 4 * D + 5].T.astype(f32)
+    gain_one, shift_one, out_shift, gain_two, shift_two = (v[None] for v in vectors)
+    router = packed[:, 4 * D + 5 : 4 * D + 5 + experts]
+    bias_cols = exp_out_bias.shape[1]
+    extra = jnp.zeros((16, D), bf).at[0].set(in_bias[0]).at[1, :bias_cols].set(exp_out_bias[0])
+    expert_pack = lax.all_gather(
+        jnp.concatenate([w_in[0], w_exp_out[0], extra], axis=0), "seq", axis=0
+    )
+    first, second = expert_pack[:, :D], expert_pack[:, D : 2 * D]
+    first_bias = expert_pack[:, 2 * D].astype(f32)
+    second_bias = expert_pack[:, 2 * D + 1, :bias_cols].reshape(1, D).astype(f32)
+    picks = expert_ids.reshape(tok, 2)
+    kept, slot = slot_ranks(priority.reshape(-1), picks, pad_mask.reshape(-1), experts, cap)
+    place = jnp.where(kept, picks * cap + slot, experts * cap)
+    where = jnp.arange(experts * cap, dtype=jnp.int32)[None]
+    spread = ((place[:, :1] == where) | (place[:, 1:] == where)).astype(bf)
+    dy_block = cotangent.reshape(tok, D)
+    dy_slots = mm(spread, dy_block, ((0,), (0,)), True).reshape(experts, cap, D)
+    dy_slots = lax.all_to_all(dy_slots, "dp", split_axis=0, concat_axis=0, tiled=True)
+    dy_slots = dy_slots.reshape(-1, D)
+    x = to_row(tokens).astype(f32)
+    dy = to_row(cotangent).astype(f32)
+    open_row = lax.all_to_all(
+        jnp.broadcast_to(pad_mask[:, None], (rows_dev, 8, pos_dev)), "seq", 0, 2, tiled=True
+    )[0, :1]
+    normed_one, inv_one = norm_stats(x)
+    h_one = (normed_one * gain_one + shift_one).astype(bf)
+    qkv = mm(h_one, qkv_weight, ((1,), (0,)), True)
+    q, k, v = (qkv[:, i * D : (i + 1) * D].reshape(-1, HEADS, HEAD) for i in range(3))
+    scale = HEAD ** (-0.5)
+    scores = jnp.einsum("qhd,khd->hqk", q, k, preferred_element_type=f32) * scale
+    scores = jnp.where((open_row > 0)[:, None], scores, -1e30)
+    weights = jnp.exp(scores - jnp.max(scores, axis=-1, keepdims=True))
+    probs = weights / jnp.sum(weights, axis=-1, keepdims=True)
+    probs_low = probs.astype(bf)
+    attended = jnp.einsum("hqk,khd->qhd", probs_low, v, preferred_element_type=f32)
+    attended = attended.astype(bf).reshape(-1, D)
+    branch = mm(attended, out_weight, ((1,), (0,))) + out_shift
+    normed_two, inv_two = norm_stats(x + branch)
+    h_two = (normed_two * gain_two + shift_two).astype(bf)
+    h_block = to_block(h_two, rows_dev).reshape(tok, D)
+    branch_block = to_block(branch.astype(bf), rows_dev).reshape(tok, D)
+    rows = mm(spread, h_block, ((0,), (0,)), True).reshape(experts, cap, D)
+    rows = lax.all_to_all(rows, "dp", split_axis=0, concat_axis=0, tiled=True).reshape(-1, D)
+    mine = lax.axis_index("dp")
+    probs_rt = jax.nn.softmax(mm(rows, router, ((1,), (0,))), axis=-1)
+    is_mine = (jnp.arange(experts) == mine).astype(f32)[None]
+    gate = jnp.sum(probs_rt * is_mine, axis=-1, keepdims=True)
+    pre = jnp.einsum("rd,qdf->qrf", rows, first, preferred_element_type=f32) + first_bias[:, None]
+    act = jax.nn.gelu(pre, approximate=False).astype(bf)
+    made = jnp.einsum("qrf,qfd->rd", act, second, preferred_element_type=f32) + second_bias
+    made = made.astype(bf).astype(f32)
+    dy_f32 = dy_slots.astype(f32)
+    grad_out = (gate * dy_f32).astype(bf)
+    grad_act = jnp.einsum("rd,qfd->qrf", grad_out, second, preferred_element_type=f32)
+    grad_pre = (grad_act * gelu_slope(pre)).astype(bf)
+    grad_gate = jnp.sum(dy_f32 * made, axis=-1, keepdims=True)
+    grad_logits = (grad_gate * gate * (is_mine - probs_rt)).astype(bf)
+    grad_rows = jnp.einsum("qrf,qdf->rd", grad_pre, first, preferred_element_type=f32)
+    grad_rows = (grad_rows + mm(grad_logits, router, ((1,), (1,)))).astype(bf)
+    grad_rows = lax.all_to_all(
+        grad_rows.reshape(experts, cap, D), "dp", split_axis=0, concat_axis=0, tiled=True
+    ).reshape(-1, D)
+    made = lax.all_to_all(
+        (gate * made).astype(bf).reshape(experts, cap, D),
+        "dp",
+        split_axis=0,
+        concat_axis=0,
+        tiled=True,
+    ).reshape(-1, D)
+    second_grad = jnp.einsum("qrf,rd->qfd", act, grad_out, preferred_element_type=f32)
+    first_grad = jnp.einsum("rd,qrf->qdf", rows, grad_pre, preferred_element_type=f32)
+    router_grad = mm(rows, grad_logits, ((0,), (0,)))
+    extra = jnp.zeros((n_seq, 16, D), f32)
+    extra = extra.at[:, 0].set(jnp.sum(grad_pre, axis=1, dtype=f32))
+    extra = extra.at[:, 1, :bias_cols].set(
+        jnp.sum(grad_out, axis=0, dtype=f32).reshape(n_seq, bias_cols)
+    )
+    expert_grads = lax.psum_scatter(
+        jnp.concatenate([first_grad, second_grad, extra], axis=1).astype(bf),
+        "seq",
+        scatter_dimension=0,
+    ).astype(f32)
+    block_output = (
+        tokens.reshape(tok, D).astype(f32)
+        + branch_block.astype(f32)
+        + mm(spread, made, ((1,), (0,)))
+    ).astype(bf)
+    grad_h2 = mm(spread, grad_rows, ((1,), (0,)), True).reshape(rows_dev, pos_dev, D)
+    grad_h2 = to_row(grad_h2).astype(f32)
+    gain_two_grad = jnp.sum(grad_h2 * normed_two, axis=0)
+    shift_two_grad = jnp.sum(grad_h2, axis=0)
+    grad_resid = dy + norm_grad(grad_h2, normed_two, inv_two, gain_two)
+    grad_branch = grad_resid.astype(bf)
+    out_weight_grad = mm(attended, grad_branch, ((0,), (0,)))
+    out_shift_grad = jnp.sum(grad_branch, axis=0, dtype=f32)
+    grad_att = mm(grad_branch, out_weight, ((1,), (1,)), True).reshape(-1, HEADS, HEAD)
+    grad_probs = jnp.einsum("qhd,khd->hqk", grad_att, v, preferred_element_type=f32)
+    delta = jnp.sum(probs * grad_probs, axis=-1, keepdims=True)
+    grad_scores = (probs * (grad_probs - delta)).astype(bf)
+    grad_q = jnp.einsum("hqk,khd->qhd", grad_scores, k, preferred_element_type=f32) * scale
+    grad_k = jnp.einsum("hqk,qhd->khd", grad_scores, q, preferred_element_type=f32) * scale
+    grad_v = jnp.einsum("hqk,qhd->khd", probs_low, grad_att, preferred_element_type=f32)
+    grad_qkv = jnp.concatenate(
+        [g.astype(bf).reshape(-1, D) for g in (grad_q, grad_k, grad_v)], axis=1
+    )
+    qkv_weight_grad = mm(h_one, grad_qkv, ((0,), (0,)))
+    grad_h1 = mm(grad_qkv, qkv_weight, ((1,), (1,)))
+    gain_one_grad = jnp.sum(grad_h1 * normed_one, axis=0)
+    shift_one_grad = jnp.sum(grad_h1, axis=0)
+    grad_x = (grad_resid + norm_grad(grad_h1, normed_one, inv_one, gain_one)).astype(bf)
+    tokens_grad = to_block(grad_x, rows_dev)
+    vectors = jnp.stack(
+        [gain_one_grad, shift_one_grad, out_shift_grad, gain_two_grad, shift_two_grad], axis=1
+    )
+    pad = jnp.zeros((D, 128 - 5 - experts), f32)
+    dense = lax.psum_scatter(
+        jnp.concatenate([qkv_weight_grad, out_weight_grad, vectors, router_grad, pad], axis=1),
+        both,
+        scatter_dimension=0,
+        tiled=True,
+    )
+    vectors = dense[:, 4 * D : 4 * D + 5].T
+    return (
+        block_output.reshape(rows_dev, pos_dev, D),
+        tokens_grad,
+        vectors[0],
+        vectors[1],
+        dense[:, : 3 * D],
+        dense[:, 3 * D : 4 * D],
+        vectors[2],
+        vectors[3],
+        vectors[4],
+        dense[:, 4 * D + 5 : 4 * D + 5 + experts],
+        expert_grads[None, :D],
+        expert_grads[None, 2 * D],
+        expert_grads[None, D : 2 * D],
+        expert_grads[None, 2 * D + 1, :bias_cols],
+    )
+
+
+def shards(*args):
+    if args[2].shape[0] == lax.axis_size("seq") and args[13].shape[0] == 1:
+        return shards_rows(*args)
+    return shards_general(*args)
+
+
 def solution(mesh):
     return jax.shard_map(
         shards,

time: 1290 us -> 762 us (0.59)
  waiting for transfers between devices: 532 us -> 350 us
  blocking collectives: 253 us -> 73.1 us
  local copies, waits for them, and re-layouts: 166 us -> 49.4 us
  other arithmetic: 141 us -> 49 us
  starting transfers between devices: 11.6 us -> 31.4 us
  matrix products: 171 us -> 184 us
    reduce_scatter x5 -> x1, waiting for transfers between devices: 351 us -> 75.5 us  [shards_rows(): lax.psum_scatter(jnp.concatenate([first_grad, second_grad, extra], axis=1...]
    all_to_all x2 -> x8, waiting for transfers between devices: 28.2 us -> 148 us  [the longest x1 52 us: shards_rows(): lax.all_to_all((gate * made).astype(bf).reshape(experts, cap, D), 'dp', s...]
    all_gather x5 -> x2, waiting for transfers between devices: 151 us -> 37.5 us  [the longest x1 37.5 us: shards_rows(): lax.all_gather(jnp.concatenate([w_qkv, w_out, vectors, w_router, pad], ax...]
    unnamed x10 -> x5, waiting for transfers between devices: 1.49 us -> 88.3 us
    unnamed x2 -> x0, blocking collectives: 82.6 us -> none
    all_gather x2 -> x0, blocking collectives: 71.6 us -> none  [the longest x1 66.2 us: shards(): lax.all_gather(w_router, ('dp', 'seq'), axis=0, tiled=True)]
    unnamed x162 -> x131, local copies, waits for them, and re-layouts: 51.4 us -> 5.16 us
    scatter-add x2 -> x0, other arithmetic: 41.7 us -> none  [the longest x1 28.2 us: shards(): jnp.zeros((tok_count, D), jnp.float32).at[token_pairs].add(grad_rows_back)]
  transfers between devices with their start and end apart: 12 -> 12, of which waited for: 11 -> 10; matrix products, arithmetic and copies ran while one was open for 12% -> 20% of each run, Pallas kernels for 0% -> 0%
where the time goes in v1:
time: 762 us; the launch traced here: 752 us
  waiting for transfers between devices  350 us (46%)
  matrix products  184 us (24%)
  blocking collectives  73.1 us (10%)
  local copies, waits for them, and re-layouts  49.4 us (6%)
  other arithmetic  49 us (6%)
  starting transfers between devices  31.4 us (4%)
  between operations  14.9 us (2%)
    unnamed x5, waiting for transfers between devices  88.3 us
    reduce_scatter x1, waiting for transfers between devices, shards_rows(): lax.psum_scatter(jnp.concatenate([first_grad, second_grad, extra], axis=1...  75.5 us
    all_to_all x1, waiting for transfers between devices, shards_rows(): lax.all_to_all((gate * made).astype(bf).reshape(experts, cap, D), 'dp', s...  52 us
    all_to_all x1, blocking collectives, shards_rows(): lax.all_to_all(grad_rows.reshape(experts, cap, D), 'dp', split_axis=0, co...  48.8 us
    dot_general x13, matrix products, mm(): lax.dot_general(a, b, (contract, ((), ())), preferred_element_type=jnp.fl...  43.3 us
    dot_general x1, matrix products, shards_rows(): jnp.einsum('rd,qdf->qrf', rows, first, preferred_element_type=f32)  41.6 us
    all_to_all x1, waiting for transfers between devices, shards_rows(): lax.all_to_all(rows, 'dp', split_axis=0, concat_axis=0, tiled=True)  39.9 us
    all_gather x1, waiting for transfers between devices, shards_rows(): lax.all_gather(jnp.concatenate([w_qkv, w_out, vectors, w_router, pad], ax...  37.5 us
  transfers between devices with their start and end apart: 12, of which 10 were waited for; matrix products, arithmetic and copies ran while one was open for 20% of the time, Pallas kernels for 0%

profile of v1, /device:TPU:0, one launch (start us, length us, event | category | flops | bytes accessed | tf_op | source)
XLA Modules:
  0.0 751.7 jit_solution(5464178582613282489)
XLA Ops:
  18.2 8.0 %all_to_all.80 = s32[4,8,144]{2,1,0:T(8,128)S(1)} all-to-all(s32[4,8,144]{2,1,0:T(8,128)S(1)} %broadcast_in_dim.39), channel_id=1, replica_groups=mesh['dp'=8,'seq'=4] {'seq'}, dimensions={0} | all-to-all | bytes 36864 | tf_op jit(solution)/shard_map/all_to_all | solution.py:405
  30.0 12.3 %all-to-all-done = bf16[4,144,768]{2,1,0:T(8,128)(2,1)S(1)} async-done(((bf16[4,144,768]{2,1,0:T(8,128)(2,1)}), bf16[4,144,768]{2,1,0:T(8,128)(2,1)S(1)}, u32[]{:S(2)}, u32[]{:S(2)}) %all-to-all-start) | async-done | bytes 884768 | tf_op jit(solution)/shard_map/all_to_all | solution.py:343
  43.2 37.5 %all-gather.4.cloned.1.call-done = bf16[768,3200]{1,0:T(8,128)(2,1)} async-done(((bf16[24,3200]{1,0:T(8,128)(2,1)}), bf16[768,3200]{1,0:T(8,128)(2,1)}) %all-gather.4.cloned.1.call-update) | async-done | bytes 4915216 | tf_op jit(solution)/shard_map/all_gather | solution.py:379
  94.4 9.7 %fusion.116 = (f32[12,576]{1,0:T(8,128)S(1)}, f32[12,576,576]{1,2,0:T(8,128)}) fusion(pred[576]{0:T(1024)(128)(4,1)S(1)} %compare_reduce_fusion, bf16[576,12,64]{0,2,1:T(8,128)(2,1)S(1)} %bitcast.203, bf16[576,12,64]{0,2,1:T(8,128)(2,1)S(1)} %bitcast.201), kind=kOutput, calls=%fused_computation.190 | convolution fusion | flops 525533760 | bytes 17722944 | tf_op jit(solution)/shard_map/sub | solution.py:415
  104.1 8.2 %fusion.65 = bf16[12,64,576]{2,1,0:T(8,128)(2,1)S(1)} fusion(bf16[576,12,64]{0,2,1:T(8,128)(2,1)} %bitcast.216, f32[12,576,576]{1,2,0:T(8,128)} %get-tuple-element.153, f32[12,576]{1,0:T(8,128)S(1)} %get-tuple-element.152), kind=kOutput, calls=%fused_computation.115 | convolution fusion | flops 518012928 | bytes 17722368 | tf_op jit(solution)/shard_map/hqk,khd->qhd/dot_general | solution.py:418
  122.8 21.3 %all-to-all-done.3 = bf16[4,144,768]{2,1,0:T(8,128)(2,1)S(1)} async-done(((bf16[4,144,768]{2,1,0:T(8,128)(2,1)}), bf16[4,144,768]{2,1,0:T(8,128)(2,1)S(1)}, u32[]{:S(2)}, u32[]{:S(2)}) %all-to-all-start.3) | async-done | bytes 884768 | tf_op jit(solution)/shard_map/all_to_all | solution.py:348
  154.9 39.9 %all-to-all-done.4 = bf16[8,152,768]{2,1,0:T(8,128)(2,1)S(1)} async-done(((bf16[8,152,768]{2,1,0:T(8,128)(2,1)}), bf16[8,152,768]{2,1,0:T(8,128)(2,1)S(1)}, u32[]{:S(2)}, u32[]{:S(2)}) %all-to-all-start.4) | async-done | bytes 1867808 | tf_op jit(solution)/shard_map/all_to_all | solution.py:426
  202.9 41.6 %fusion.3 = (bf16[4,1216,768]{2,1,0:T(8,128)(2,1)}, f32[4,768,1216]{1,2,0:T(8,128)}) fusion(f32[4,768]{1,0:T(4,128)S(1)} %bitcast.228, bf16[1216,768,1]{1,0,2:T(8,128)(2,1)S(1)} %bitcast.196, bf16[4,1552,768]{2,1,0:T(8,128)(2,1)} %bitcast.237), kind=kOutput, calls=%fused_computation.9 | convolution fusion | flops 5984354304 | bytes 29011968 | tf_op jit(solution)/shard_map/rd,qdf->qrf/dot_general | solution.py:431
  245.4 14.8 %fusion.49 = (f32[1216]{0:T(1024)S(1)}, f32[1216,768]{1,0:T(8,128)S(1)}, bf16[1216,768]{1,0:T(8,128)(2,1)}) fusion(bf16[1216,768]{1,0:T(8,128)(2,1)} %bitcast.159, f32[1216]{0:T(1024)S(1)} %multiply_reduce_fusion.7, f32[768]{0:T(1024)S(1)} %reshape.420, bf16[4,1216,768]{2,1,0:T(8,128)(2,1)} %get-tuple-element.154, bf16[4,1552,768]{2,1,0:T(8,128)(2,1)} %bitcast.239), kind=kOutput, calls=%fused_computation.66 | convolution fusion | flops 5745277952 | bytes 19673600 | tf_op jit(solution)/shard_map/qrf,qfd->rd/dot_general | solution.py:433
  260.2 15.1 %convert_reduce_fusion = (bf16[4,768]{1,0:T(4,128)(2,1)}, bf16[4,1216,768]{2,1,0:T(8,128)(2,1)S(1)}) fusion(f32[4,768,1216]{1,2,0:T(8,128)} %get-tuple-element.155, f32[4,768]{1,0:T(4,128)S(1)} %bitcast.229, f32[1216,768]{1,0:T(8,128)S(1)} %get-tuple-element.141, f32[1216]{0:T(1024)S(1)} %multiply_reduce_fusion.7, bf16[4,1552,768]{2,1,0:T(8,128)(2,1)S(1)} %bitcast.240), kind=kOutput, calls=%fused_computation.23 | convolution fusion | flops 5788234752 | bytes 30894080 | tf_op jit(solution)/shard_map/rd,qfd->qrf/dot_general | solution.py:437
  283.2 48.8 %all_to_all.81 = bf16[8,152,768]{2,1,0:T(8,128)(2,1)S(1)} all-to-all(bf16[8,152,768]{2,1,0:T(8,128)(2,1)S(1)} %bitcast.200), channel_id=1, replica_groups=mesh['dp'=8,'seq'=4] {'dp'}, dimensions={0} | all-to-all | bytes 3735552 | tf_op jit(solution)/shard_map/all_to_all | solution.py:443
  341.4 9.5 %all-to-all-done.9 = bf16[4,144,768]{2,1,0:T(8,128)(2,1)S(1)} async-done(((bf16[4,144,768]{2,1,0:T(8,128)(2,1)}), bf16[4,144,768]{2,1,0:T(8,128)(2,1)S(1)}, u32[]{:S(2)}, u32[]{:S(2)}) %all-to-all-start.9) | async-done | bytes 884768 | tf_op jit(solution)/shard_map/all_to_all | solution.py:343
  373.1 11.1 %multiply_reduce_fusion = (f32[12,576]{1,0:T(8,128)S(1)}, f32[12,576,576]{1,2,0:T(8,128)}) fusion(f32[12,576,576]{1,2,0:T(8,128)} %get-tuple-element.153, f32[12,576]{1,0:T(8,128)S(1)} %copy-done.32, bf16[576,12,64]{0,2,1:T(8,128)(2,1)S(1)} %bitcast.218, bf16[576,12,64]{0,2,1:T(8,128)(2,1)S(1)} %bitcast.217), kind=kOutput, calls=%fused_computation.4 | convolution fusion | flops 521544960 | bytes 33675264 | tf_op jit(solution)/shard_map/qhd,khd->hqk/dot_general | solution.py:480
  384.2 12.3 %multiply_convert_fusion = bf16[12,576,576]{1,2,0:T(8,128)(2,1)S(1)} fusion(f32[12,576,576]{1,2,0:T(8,128)} %get-tuple-element.161, f32[12,576]{1,0:T(8,128)S(1)} %get-tuple-element.160, f32[12,576,576]{1,2,0:T(8,128)} %get-tuple-element.153, f32[12,576]{1,0:T(8,128)S(1)} %copy-done.32), kind=kLoop, calls=%fused_computation.3 | loop fusion | flops 15925248 | bytes 39868416 | tf_op jit(solution)/shard_map/convert_element_type | solution.py:482
  400.9 9.9 %fusion.68 = bf16[12,64,576]{2,1,0:T(8,128)(2,1)} fusion(bf16[576,12,64]{0,2,1:T(8,128)(2,1)S(1)} %bitcast.219, f32[12,576,576]{1,2,0:T(8,128)} %get-tuple-element.153, f32[12,576]{1,0:T(8,128)S(1)} %copy-done.32), kind=kOutput, calls=%fused_computation.116 | convolution fusion | flops 518012928 | bytes 17722368 | tf_op jit(solution)/shard_map/hqk,qhd->khd/dot_general | solution.py:485
  430.2 11.5 %concatenate.28 = f32[768,3200]{1,0:T(8,128)} concatenate(f32[768,2304]{1,0:T(8,128)} %fusion.71, f32[768,768]{1,0:T(8,128)S(1)} %fusion.108, f32[768,1]{1,0:T(8,128)} %stack.48, f32[768,1]{1,0:T(8,128)} %stack.49, f32[768,1]{1,0:T(8,128)} %stack.50, f32[768,1]{1,0:T(8,128)} %stack.51, f32[768,1]{1,0:T(8,128)} %stack.52, f32[768,8]{1,0:T(8,128)} %fusion.118, ...), dimensions={1} | concatenate | bytes 19660800 | tf_op jit(solution)/shard_map/concatenate | solution.py:500
  444.3 10.5 %convert_bitcast_fusion = bf16[4,768,768]{2,1,0:T(8,128)(2,1)S(1)} fusion(bf16[4,1216,768]{2,1,0:T(8,128)(2,1)} %copy-done.58, bf16[1216,768,1]{1,0,2:T(8,128)(2,1)S(1)} %bitcast.198), kind=kOutput, calls=%fused_computation.46 | convolution fusion | flops 5740167168 | bytes 14057472 | tf_op jit(solution)/shard_map/rd,qrf->qdf/dot_general | solution.py:454
  454.9 9.2 %convolution_convert_fusion.3 = bf16[4,768,768]{2,1,0:T(8,128)(2,1)S(1)} fusion(bf16[4,1216,768]{2,1,0:T(8,128)(2,1)} %get-tuple-element.154, f32[1216,768]{1,0:T(8,128)S(1)} %copy-done.60, f32[1216]{0:T(1024)S(1)} %multiply_reduce_fusion.7), kind=kOutput, calls=%fused_computation.81 | convolution fusion | flops 5742034944 | bytes 15930112 | tf_op jit(solution)/shard_map/qrf,rd->qfd/dot_general | solution.py:453
  464.1 9.9 %pad_maximum_fusion = bf16[4,1552,768]{2,1,0:T(8,128)(2,1)} fusion(bf16[4,16,768]{2,1,0:T(8,128)(2,1)S(1)} %scatter.19, bf16[4,768,768]{2,1,0:T(8,128)(2,1)S(1)} %convolution_convert_fusion.3, bf16[4,768,768]{2,1,0:T(8,128)(2,1)S(1)} %convert_bitcast_fusion), kind=kLoop, calls=%fused_computation.41 | loop fusion | flops 28606464 | bytes 19070976 | tf_op jit(solution)/shard_map/concatenate | solution.py:462
  474.0 16.3 %all_to_all.82 = bf16[4,144,768]{2,1,0:T(8,128)(2,1)S(1)} all-to-all(bf16[4,144,768]{2,1,0:T(8,128)(2,1)} %bitcast.223), channel_id=1, replica_groups=mesh['dp'=8,'seq'=4] {'seq'}, dimensions={0} | all-to-all | bytes 1769472 | tf_op jit(solution)/shard_map/all_to_all | solution.py:348
  498.4 52.0 %all-to-all-done.5 = bf16[8,152,768]{2,1,0:T(8,128)(2,1)} async-done(((bf16[8,152,768]{2,1,0:T(8,128)(2,1)}), bf16[8,152,768]{2,1,0:T(8,128)(2,1)}, u32[]{:S(2)}, u32[]{:S(2)}) %all-to-all-start.5) | async-done | bytes 1867808 | tf_op jit(solution)/shard_map/all_to_all | solution.py:446
  559.5 8.3 %all-to-all-done.10 = bf16[4,144,768]{2,1,0:T(8,128)(2,1)S(1)} async-done(((bf16[4,144,768]{2,1,0:T(8,128)(2,1)}), bf16[4,144,768]{2,1,0:T(8,128)(2,1)S(1)}, u32[]{:S(2)}, u32[]{:S(2)}) %all-to-all-start.10) | async-done | bytes 884768 | tf_op jit(solution)/shard_map/all_to_all | solution.py:348
  567.9 88.2 %all-reduce.6.cloned.1.call-done = f32[768,3200]{1,0:T(8,128)} async-done(((f32[768,3200]{1,0:T(8,128)}), f32[768,3200]{1,0:T(8,128)}) %all-reduce.6.cloned.1.call-update) | async-done | bytes 9830416
  662.3 75.5 %reduce-scatter.2.cloned.1.call-done = bf16[1,1552,768]{2,1,0:T(8,128)(2,1)} async-done(((bf16[4,1552,768]{2,1,0:T(8,128)(2,1)}), bf16[1,1552,768]{2,1,0:T(8,128)(2,1)}) %reduce-scatter.2.cloned.1.call-update) | async-done | bytes 2383888 | tf_op jit(solution)/shard_map/reduce_scatter | solution.py:461
  (253 shorter events, 155.4 us)
Async XLA Ops:
  7.2 73.5 %all-gather.4.cloned.1.call-start = ((), (), s32[]{:S(2)}) async-start(), calls=%async_computation.12 | async-start | bytes 5068800 | tf_op jit(solution)/shard_map/all_gather | solution.py:379
  13.4 188.7 %all-gather.6.cloned.1.call-start = ((), (), s32[]{:S(2)}) async-start(), calls=%async_computation.14 | async-start | bytes 11919360 | tf_op jit(solution)/shard_map/all_gather | solution.py:388
  26.2 16.2 %all-to-all-start = ((bf16[4,144,768]{2,1,0:T(8,128)(2,1)}), bf16[4,144,768]{2,1,0:T(8,128)(2,1)S(1)}, u32[]{:S(2)}, u32[]{:S(2)}) async-start(bf16[4,144,768]{2,1,0:T(8,128)(2,1)} %param.25), calls=%async_computation | async-start | bytes 1769472 | tf_op jit(solution)/shard_map/all_to_all | solution.py:343
  42.3 69.9 %copy-start.4 = (bf16[4,144,768]{2,1,0:T(8,128)(2,1)}, bf16[4,144,768]{2,1,0:T(8,128)(2,1)S(1)}, u32[]{:S(2)}) copy-start(bf16[4,144,768]{2,1,0:T(8,128)(2,1)S(1)} %all-to-all-done) | copy-start | bytes 2654212
  42.7 40.4 %copy-start.35 = (f32[576]{0:T(1024)}, f32[576]{0:T(1024)S(1)}, u32[]{:S(2)}) copy-start(f32[576]{0:T(1024)S(1)} %div.45) | copy-start | bytes 6916
  43.2 39.9 %copy-start.37 = (f32[576]{0:T(1024)}, f32[576]{0:T(1024)S(1)}, u32[]{:S(2)}) copy-start(f32[576]{0:T(1024)S(1)} %rsqrt.20) | copy-start | bytes 6916
  82.6 33.7 %copy-start.26 = (f32[768]{0:T(1024)}, f32[768]{0:T(1024)S(1)}, u32[]{:S(2)}) copy-start(f32[768]{0:T(1024)S(1)} %get-tuple-element.126) | copy-start | bytes 9220
  115.8 31.5 %copy-start = (f32[576,768]{1,0:T(8,128)}, f32[576,768]{1,0:T(8,128)S(1)}, u32[]{:S(2)}) copy-start(f32[576,768]{1,0:T(8,128)S(1)} %get-tuple-element.150) | copy-start | bytes 5308420
  117.6 26.4 %all-to-all-start.3 = ((bf16[4,144,768]{2,1,0:T(8,128)(2,1)}), bf16[4,144,768]{2,1,0:T(8,128)(2,1)S(1)}, u32[]{:S(2)}, u32[]{:S(2)}) async-start(bf16[4,144,768]{2,1,0:T(8,128)(2,1)} %bitcast.21), calls=%async_computation.3 | async-start | bytes 1769472 | tf_op jit(solution)/shard_map/all_to_all | solution.py:348
  122.7 28.9 %copy-start.49 = (s32[576]{0:T(1024)}, s32[576]{0:T(1024)S(1)}, u32[]{:S(2)}) copy-start(s32[576]{0:T(1024)S(1)} %get-tuple-element.136) | copy-start | bytes 6916
  147.3 47.4 %all-to-all-start.4 = ((bf16[8,152,768]{2,1,0:T(8,128)(2,1)}), bf16[8,152,768]{2,1,0:T(8,128)(2,1)S(1)}, u32[]{:S(2)}, u32[]{:S(2)}) async-start(bf16[8,152,768]{2,1,0:T(8,128)(2,1)} %bitcast.210), calls=%async_computation.4 | async-start | bytes 3735552 | tf_op jit(solution)/shard_map/all_to_all | solution.py:426
  151.6 49.2 %copy-start.46 = (f32[8]{0:T(128)}, f32[8]{0:T(128)S(1)}, u32[]{:S(2)}) copy-start(f32[8]{0:T(128)S(1)} %compare_convert_fusion) | copy-start | bytes 100
  194.8 49.7 %copy-start.2 = (bf16[8,152,768]{2,1,0:T(8,128)(2,1)}, bf16[8,152,768]{2,1,0:T(8,128)(2,1)S(1)}, u32[]{:S(2)}) copy-start(bf16[8,152,768]{2,1,0:T(8,128)(2,1)S(1)} %all-to-all-done.4) | copy-start | bytes 5603332
  194.8 50.6 %all-to-all-start.7 = ((bf16[8,152,768]{2,1,0:T(8,128)(2,1)}), bf16[8,152,768]{2,1,0:T(8,128)(2,1)}, u32[]{:S(2)}, u32[]{:S(2)}) async-start(bf16[8,152,768]{2,1,0:T(8,128)(2,1)} %bitcast.209), calls=%async_computation.7 | async-start | bytes 3735552 | tf_op jit(solution)/shard_map/all_to_all | solution.py:401
  281.5 50.5 %copy-start.50 = (s32[576]{0:T(1024)S(1)}, s32[576]{0:T(1024)}, u32[]{:S(2)}) copy-start(s32[576]{0:T(1024)} %copy-done.49) | copy-start | bytes 6916
  281.5 50.5 %copy-start.53 = (s32[576]{0:T(1024)S(1)}, s32[576]{0:T(1024)}, u32[]{:S(2)}) copy-start(s32[576]{0:T(1024)} %copy-done.52) | copy-start | bytes 6916
  334.6 16.3 %all-to-all-start.9 = ((bf16[4,144,768]{2,1,0:T(8,128)(2,1)}), bf16[4,144,768]{2,1,0:T(8,128)(2,1)S(1)}, u32[]{:S(2)}, u32[]{:S(2)}) async-start(bf16[4,144,768]{2,1,0:T(8,128)(2,1)} %bitcast.43), calls=%async_computation.9 | async-start | bytes 1769472 | tf_op jit(solution)/shard_map/all_to_all | solution.py:343
  350.9 16.2 %all-to-all-start.6 = ((bf16[4,144,768]{2,1,0:T(8,128)(2,1)}), bf16[4,144,768]{2,1,0:T(8,128)(2,1)S(1)}, u32[]{:S(2)}, u32[]{:S(2)}) async-start(bf16[4,144,768]{2,1,0:T(8,128)(2,1)} %param.26), calls=%async_computation.6 | async-start | bytes 1769472 | tf_op jit(solution)/shard_map/all_to_all | solution.py:343
  354.4 301.7 %all-reduce.6.cloned.1.call-start = ((), (), s32[]{:S(2)}) async-start(), calls=%async_computation.15 | async-start | bytes 19660800
  441.7 296.1 %reduce-scatter.2.cloned.1.call-start = ((), (), s32[]{:S(2)}) async-start(), calls=%async_computation.13 | async-start | bytes 11919360 | tf_op jit(solution)/shard_map/reduce_scatter | solution.py:461
  490.3 60.1 %all-to-all-start.5 = ((bf16[8,152,768]{2,1,0:T(8,128)(2,1)}), bf16[8,152,768]{2,1,0:T(8,128)(2,1)}, u32[]{:S(2)}, u32[]{:S(2)}) async-start(bf16[8,152,768]{2,1,0:T(8,128)(2,1)} %bitcast.208), calls=%async_computation.5 | async-start | bytes 3735552 | tf_op jit(solution)/shard_map/all_to_all | solution.py:446
  495.4 60.0 %copy-start.51 = (s32[576]{0:T(1024)S(1)}, s32[576]{0:T(1024)}, u32[]{:S(2)}) copy-start(s32[576]{0:T(1024)} %copy-done.49) | copy-start | bytes 6916
  498.4 57.0 %copy-start.54 = (s32[576]{0:T(1024)S(1)}, s32[576]{0:T(1024)}, u32[]{:S(2)}) copy-start(s32[576]{0:T(1024)} %copy-done.52) | copy-start | bytes 6916
  550.4 17.5 %all-to-all-start.10 = ((bf16[4,144,768]{2,1,0:T(8,128)(2,1)}), bf16[4,144,768]{2,1,0:T(8,128)(2,1)S(1)}, u32[]{:S(2)}, u32[]{:S(2)}) async-start(bf16[4,144,768]{2,1,0:T(8,128)(2,1)} %bitcast.205), calls=%async_computation.10 | async-start | bytes 1769472 | tf_op jit(solution)/shard_map/all_to_all | solution.py:348
  (51 other events, 498.4 us)
Sparse Core Ops, SparseCore 0:
  13.5 67.0 all-gather.3
  82.2 73.0 all-gather.5
  441.8 214.2 all-reduce.5
  658.7 79.0 reduce-scatter.1

commit v2 on v1

--- a/solution.py
+++ b/solution.py
@@ -1,6 +1,10 @@
+import functools
+
 import jax
 import jax.numpy as jnp
 from jax import lax
+from jax.experimental import pallas as pl
+from jax.experimental.pallas import tpu as pltpu
 from jax.sharding import PartitionSpec as P
 
 D = 768
@@ -318,6 +322,227 @@
     )
 
 
+MESH = pl.DeviceIdType.MESH
+VMEM = pl.BlockSpec(memory_space=pltpu.VMEM)
+ANY = pl.BlockSpec(memory_space=pl.ANY)
+ERF = (0.1274147955, -0.142248368, 0.7107068705, -0.7265760135, 0.5307027145)
+
+
+def nn(a, b):
+    return lax.dot_general(a, b, (((1,), (0,)), ((), ())), preferred_element_type=jnp.float32)
+
+
+def nt(a, b):
+    return lax.dot_general(a, b, (((1,), (1,)), ((), ())), preferred_element_type=jnp.float32)
+
+
+def tn(a, b):
+    return lax.dot_general(a, b, (((0,), (0,)), ((), ())), preferred_element_type=jnp.float32)
+
+
+def gelu_parts(v):
+    bell = jnp.exp(v * v * -0.5)
+    t = 1.0 / (jnp.abs(v) * (0.3275911 * 0.7071067811865476) + 1.0)
+    a, b, c, d, e = ERF
+    tail = ((((e * t + d) * t + c) * t + b) * t + a) * t * bell
+    cdf = jnp.where(v < 0.0, tail, 1.0 - tail)
+    return v * cdf, cdf + v * (bell * 0.3989422804014327)
+
+
+def other(me, step):
+    bit = lambda k: lax.rem(me // k + step // k, 2) * k
+    return bit(4) + bit(2) + bit(1)
+
+
+def moe_kernel(
+    experts,
+    h_ref,
+    into_ref,
+    from_ref,
+    dy_ref,
+    first_any,
+    second_any,
+    bias1_ref,
+    bias2_ref,
+    router_ref,
+    grad_ref,
+    outs_ref,
+    first_grad_ref,
+    second_grad_ref,
+    router_grad_ref,
+    bias1_grad_ref,
+    bias2_grad_ref,
+    sent,
+    rows,
+    rows_t,
+    go,
+    act,
+    gp,
+    back_sent,
+    back,
+    logit_grad,
+    first,
+    second,
+    w_sem,
+    send_sem,
+    recv_sem,
+    send_sem2,
+    recv_sem2,
+):
+    n = experts
+    cap = dy_ref.shape[0] // n
+    bf, f32 = jnp.bfloat16, jnp.float32
+    blocks = first.shape[0]
+    me, seq = lax.axis_index("dp"), lax.axis_index("seq")
+    barrier = pltpu.get_barrier_semaphore()
+    for step in range(1, n):
+        pl.semaphore_signal(barrier, inc=1, device_id=(other(me, step), seq), device_id_type=MESH)
+    load1 = pltpu.make_async_copy(first_any, first, w_sem.at[0])
+    load2 = pltpu.make_async_copy(second_any, second, w_sem.at[1])
+    load1.start()
+    load2.start()
+    at = lambda i: pl.ds(pl.multiple_of(i * cap, cap), cap)
+    pl.semaphore_wait(barrier, n - 1)
+
+    def dispatch(step, source, target, sems):
+        to = other(me, step)
+        return pltpu.make_async_remote_copy(
+            source.at[at(to)],
+            target.at[at(me)],
+            sems[0].at[step],
+            sems[1].at[step],
+            device_id=(to, seq),
+            device_id_type=MESH,
+        )
+
+    out_sems, back_sems = (send_sem, recv_sem), (send_sem2, recv_sem2)
+
+    @pl.loop(0, n - 1)
+    def _(i):
+        step = n - 1 - i
+        to = other(me, step)
+        sent[at(to), :] = nn(into_ref[at(to), :], h_ref[...]).astype(bf)
+        dispatch(step, sent, rows, out_sems).start()
+
+    rows[at(me), :] = nn(into_ref[at(me), :], h_ref[...]).astype(bf)
+    load1.wait()
+    load2.wait()
+    lane = lax.broadcasted_iota(jnp.int32, (cap, 128), 1)
+
+    @pl.loop(0, n)
+    def _(step):
+        peer = other(me, step)
+
+        @pl.when(step > 0)
+        def _():
+            dispatch(step, sent, rows, out_sems).wait_recv()
+
+        x = rows[at(peer), :]
+        dy = dy_ref[at(peer), :].astype(f32)
+        logits = jnp.where(lane < n, nn(x, router_ref[...]), -1e30)
+        probs = jnp.exp(logits - jnp.max(logits, axis=-1, keepdims=True))
+        probs = probs / jnp.sum(probs, axis=-1, keepdims=True)
+        mine = (lane == me).astype(f32)
+        gate = jnp.sum(probs * mine, axis=-1, keepdims=True)
+        grad_out = (gate * dy).astype(bf)
+        go[at(peer), :] = grad_out
+
+        def block(q, sums):
+            out, grad_row = sums
+            value, slope = gelu_parts(nn(x, first[q]) + bias1_ref[q])
+            value = value.astype(bf)
+            act[q, at(peer), :] = value
+            grad_pre = (nt(grad_out, second[q]) * slope).astype(bf)
+            gp[q, at(peer), :] = grad_pre
+            return out + nn(value, second[q]), grad_row + nt(grad_pre, first[q])
+
+        zero = jnp.zeros((cap, x.shape[1]), f32)
+        out, grad_row = lax.fori_loop(0, blocks, block, (zero, zero))
+        made = (out + bias2_ref[...]).astype(bf).astype(f32)
+        grad_gate = jnp.sum(dy * made, axis=-1, keepdims=True)
+        grad_logits = (grad_gate * gate * (mine - probs)).astype(bf)
+        logit_grad[at(peer), :] = grad_logits
+        grad_row = (grad_row + nt(grad_logits, router_ref[...])).astype(bf)
+        outs_ref[at(peer), :] = (gate * made).astype(bf)
+
+        @pl.when(step > 0)
+        def _():
+            back_sent[at(peer), :] = grad_row
+            dispatch(step, back_sent, back, back_sems).start()
+
+        @pl.when(step == 0)
+        def _():
+            back[at(peer), :] = grad_row
+
+    rows_t[...] = rows[...].T
+    ones = jnp.ones((8, rows.shape[0]), bf)
+
+    @pl.loop(0, blocks)
+    def _(q):
+        first_grad_ref[q] = nn(rows_t[...], gp[q]).astype(bf)
+        second_grad_ref[q] = tn(act[q], go[...]).astype(bf)
+        bias1_grad_ref[q] = nn(ones, gp[q])
+
+    bias2_grad_ref[...] = nn(ones, go[...])
+    router_grad_ref[...] = nn(rows_t[...], logit_grad[...])
+
+    @pl.loop(1, n)
+    def _(step):
+        dispatch(step, back_sent, back, back_sems).wait()
+        dispatch(step, sent, rows, out_sems).wait_send()
+
+    grad_ref[...] = nn(from_ref[...], back[...]).astype(bf)
+
+
+def moe(h_block, into, outof, dy_slots, first, second, bias1, bias2, router, experts):
+    bf, f32 = jnp.bfloat16, jnp.float32
+    tok, width = h_block.shape
+    slots = into.shape[0]
+    blocks, hidden = first.shape[0], first.shape[2]
+    sds = jax.ShapeDtypeStruct
+    dma = pltpu.SemaphoreType.DMA
+    big = (slots, width)
+    return pl.pallas_call(
+        functools.partial(moe_kernel, experts),
+        out_shape=(
+            sds((tok, width), bf),
+            sds(big, bf),
+            sds(first.shape, bf),
+            sds(second.shape, bf),
+            sds((width, 128), f32),
+            sds((blocks, 8, hidden), f32),
+            sds((8, width), f32),
+        ),
+        in_specs=[VMEM] * 4 + [ANY] * 2 + [VMEM] * 3,
+        out_specs=(VMEM,) * 7,
+        scratch_shapes=[
+            pltpu.VMEM(big, bf),
+            pltpu.VMEM(big, bf),
+            pltpu.VMEM((width, slots), bf),
+            pltpu.VMEM(big, bf),
+            pltpu.VMEM((blocks, slots, hidden), bf),
+            pltpu.VMEM((blocks, slots, hidden), bf),
+            pltpu.VMEM(big, bf),
+            pltpu.VMEM(big, bf),
+            pltpu.VMEM((slots, 128), bf),
+            pltpu.VMEM(first.shape, bf),
+            pltpu.VMEM(second.shape, bf),
+            dma((2,)),
+            dma((experts,)),
+            dma((experts,)),
+            dma((experts,)),
+            dma((experts,)),
+        ],
+        compiler_params=pltpu.CompilerParams(
+            collective_id=1, has_side_effects=True, vmem_limit_bytes=61 * 2**20
+        ),
+        cost_estimate=pl.CostEstimate(
+            flops=12 * slots * width * hidden * blocks, bytes_accessed=4 * 10**7, transcendentals=slots * hidden * blocks
+        ),
+        name="moe",
+    )(h_block, into, outof, dy_slots, first, second, bias1, bias2, router)
+
+
 def mm(a, b, contract, low=False):
     out = lax.dot_general(a, b, (contract, ((), ())), preferred_element_type=jnp.float32)
     return out.astype(jnp.bfloat16) if low else out
@@ -391,13 +616,15 @@
     first, second = expert_pack[:, :D], expert_pack[:, D : 2 * D]
     first_bias = expert_pack[:, 2 * D].astype(f32)
     second_bias = expert_pack[:, 2 * D + 1, :bias_cols].reshape(1, D).astype(f32)
+    held = -(-cap // 16) * 16
     picks = expert_ids.reshape(tok, 2)
     kept, slot = slot_ranks(priority.reshape(-1), picks, pad_mask.reshape(-1), experts, cap)
-    place = jnp.where(kept, picks * cap + slot, experts * cap)
-    where = jnp.arange(experts * cap, dtype=jnp.int32)[None]
-    spread = ((place[:, :1] == where) | (place[:, 1:] == where)).astype(bf)
-    dy_block = cotangent.reshape(tok, D)
-    dy_slots = mm(spread, dy_block, ((0,), (0,)), True).reshape(experts, cap, D)
+    place = jnp.where(kept, picks * held + slot, experts * held)
+    where = jnp.arange(experts * held, dtype=jnp.int32)
+    outof = ((place[:, :1] == where[None]) | (place[:, 1:] == where[None])).astype(bf)
+    place = place.T
+    into = ((place[:1] == where[:, None]) | (place[1:] == where[:, None])).astype(bf)
+    dy_slots = mm(into, cotangent.reshape(tok, D), ((1,), (0,)), True).reshape(experts, held, D)
     dy_slots = lax.all_to_all(dy_slots, "dp", split_axis=0, concat_axis=0, tiled=True)
     dy_slots = dy_slots.reshape(-1, D)
     x = to_row(tokens).astype(f32)
@@ -422,54 +649,32 @@
     h_two = (normed_two * gain_two + shift_two).astype(bf)
     h_block = to_block(h_two, rows_dev).reshape(tok, D)
     branch_block = to_block(branch.astype(bf), rows_dev).reshape(tok, D)
-    rows = mm(spread, h_block, ((0,), (0,)), True).reshape(experts, cap, D)
-    rows = lax.all_to_all(rows, "dp", split_axis=0, concat_axis=0, tiled=True).reshape(-1, D)
-    mine = lax.axis_index("dp")
-    probs_rt = jax.nn.softmax(mm(rows, router, ((1,), (0,))), axis=-1)
-    is_mine = (jnp.arange(experts) == mine).astype(f32)[None]
-    gate = jnp.sum(probs_rt * is_mine, axis=-1, keepdims=True)
-    pre = jnp.einsum("rd,qdf->qrf", rows, first, preferred_element_type=f32) + first_bias[:, None]
-    act = jax.nn.gelu(pre, approximate=False).astype(bf)
-    made = jnp.einsum("qrf,qfd->rd", act, second, preferred_element_type=f32) + second_bias
-    made = made.astype(bf).astype(f32)
-    dy_f32 = dy_slots.astype(f32)
-    grad_out = (gate * dy_f32).astype(bf)
-    grad_act = jnp.einsum("rd,qfd->qrf", grad_out, second, preferred_element_type=f32)
-    grad_pre = (grad_act * gelu_slope(pre)).astype(bf)
-    grad_gate = jnp.sum(dy_f32 * made, axis=-1, keepdims=True)
-    grad_logits = (grad_gate * gate * (is_mine - probs_rt)).astype(bf)
-    grad_rows = jnp.einsum("qrf,qdf->rd", grad_pre, first, preferred_element_type=f32)
-    grad_rows = (grad_rows + mm(grad_logits, router, ((1,), (1,)))).astype(bf)
-    grad_rows = lax.all_to_all(
-        grad_rows.reshape(experts, cap, D), "dp", split_axis=0, concat_axis=0, tiled=True
-    ).reshape(-1, D)
+    wide_router = jnp.pad(router, ((0, 0), (0, 128 - experts)))
+    grad_h2, made, first_grad, second_grad, router_grad, bias1_grad, bias2_grad = moe(
+        h_block, into, outof, dy_slots, first, second, first_bias[:, None], second_bias, wide_router, experts
+    )
     made = lax.all_to_all(
-        (gate * made).astype(bf).reshape(experts, cap, D),
+        made.reshape(experts, held, D),
         "dp",
         split_axis=0,
         concat_axis=0,
         tiled=True,
     ).reshape(-1, D)
-    second_grad = jnp.einsum("qrf,rd->qfd", act, grad_out, preferred_element_type=f32)
-    first_grad = jnp.einsum("rd,qrf->qdf", rows, grad_pre, preferred_element_type=f32)
-    router_grad = mm(rows, grad_logits, ((0,), (0,)))
-    extra = jnp.zeros((n_seq, 16, D), f32)
-    extra = extra.at[:, 0].set(jnp.sum(grad_pre, axis=1, dtype=f32))
-    extra = extra.at[:, 1, :bias_cols].set(
-        jnp.sum(grad_out, axis=0, dtype=f32).reshape(n_seq, bias_cols)
-    )
+    extra = jnp.zeros((n_seq, 16, D), f32).at[:, 0].set(bias1_grad[:, 0])
+    extra = extra.at[:, 1, :bias_cols].set(bias2_grad[0].reshape(n_seq, bias_cols))
+    extra = extra.astype(bf)
+    router_grad = router_grad[:, :experts]
     expert_grads = lax.psum_scatter(
-        jnp.concatenate([first_grad, second_grad, extra], axis=1).astype(bf),
+        jnp.concatenate([first_grad, second_grad, extra], axis=1),
         "seq",
         scatter_dimension=0,
     ).astype(f32)
     block_output = (
         tokens.reshape(tok, D).astype(f32)
         + branch_block.astype(f32)
-        + mm(spread, made, ((1,), (0,)))
+        + mm(outof, made, ((1,), (0,)))
     ).astype(bf)
-    grad_h2 = mm(spread, grad_rows, ((1,), (0,)), True).reshape(rows_dev, pos_dev, D)
-    grad_h2 = to_row(grad_h2).astype(f32)
+    grad_h2 = to_row(grad_h2.reshape(rows_dev, pos_dev, D)).astype(f32)
     gain_two_grad = jnp.sum(grad_h2 * normed_two, axis=0)
     shift_two_grad = jnp.sum(grad_h2, axis=0)
     grad_resid = dy + norm_grad(grad_h2, normed_two, inv_two, gain_two)
@@ -522,7 +727,8 @@
 
 
 def shards(*args):
-    if args[2].shape[0] == lax.axis_size("seq") and args[13].shape[0] == 1:
+    block_rows, local_experts, n_dp = args[2].shape[0], args[13].shape[0], lax.axis_size("dp")
+    if block_rows == lax.axis_size("seq") and local_experts == 1 and n_dp == 8:
         return shards_rows(*args)
     return shards_general(*args)
 

time: 762 us -> 728 us (0.955)
  matrix products: 184 us -> 75.9 us
  Pallas kernels: 0 us -> 99.6 us
  blocking collectives: 73.1 us -> 33.9 us
  local copies, waits for them, and re-layouts: 49.4 us -> 59.1 us
    pallas_call x0 -> x1, Pallas kernels: none -> 99.6 us  [moe(): pl.pallas_call(functools.partial(moe_kernel, experts), out_shape=(sds((to...]
    dot_general x6 -> x0, matrix products: 97.3 us -> none  [the longest x1 41.6 us: shards_rows(): jnp.einsum('rd,qdf->qrf', rows, first, preferred_element_type=f32)]
    all_to_all x2 -> x1, blocking collectives: 56.7 us -> 17 us  [to_row(): lax.all_to_all(block, 'seq', split_axis=0, concat_axis=1, tiled=True)[0]]
    all_to_all x2, waiting for transfers between devices: 91.8 us -> 56.3 us  [the longest x1 55.3 us: shards_rows(): lax.all_to_all(made.reshape(experts, held, D), 'dp', split_axis=0, concat...]
    all_gather x1, waiting for transfers between devices: 0.02 us -> 24 us  [shards_rows(): lax.all_gather(jnp.concatenate([w_in[0], w_exp_out[0], extra], axis=0), '...]
    all_gather x1, waiting for transfers between devices: 37.5 us -> 56.6 us  [shards_rows(): lax.all_gather(jnp.concatenate([w_qkv, w_out, vectors, w_router, pad], ax...]
    unnamed x5, waiting for transfers between devices: 88.3 us -> 104 us
    all_to_all x3 -> x2, waiting for transfers between devices: 26.8 us -> 14.5 us  [to_row(): lax.all_to_all(block, 'seq', split_axis=0, concat_axis=1, tiled=True)[0]]
  transfers between devices with their start and end apart: 12 -> 11, of which waited for: 10 -> 10; matrix products, arithmetic and copies ran while one was open for 20% -> 13% of each run, Pallas kernels for 0% -> 0%
where the time goes in v2:
time: 728 us; the launch traced here: 722 us
  waiting for transfers between devices  354 us (49%)
  Pallas kernels  99.6 us (14%)
  matrix products  75.9 us (10%)
  local copies, waits for them, and re-layouts  59.1 us (8%)
  other arithmetic  48.9 us (7%)
  starting transfers between devices  36 us (5%)
  blocking collectives  33.9 us (5%)
  between operations  14.7 us (2%)
    unnamed x5, waiting for transfers between devices  104 us
    pallas_call x1, Pallas kernels, moe(): pl.pallas_call(functools.partial(moe_kernel, experts), out_shape=(sds((to...  99.6 us
    reduce_scatter x1, waiting for transfers between devices, shards_rows(): lax.psum_scatter(jnp.concatenate([first_grad, second_grad, extra], axis=1...  75.5 us
    all_gather x1, waiting for transfers between devices, shards_rows(): lax.all_gather(jnp.concatenate([w_qkv, w_out, vectors, w_router, pad], ax...  56.6 us
    all_to_all x1, waiting for transfers between devices, shards_rows(): lax.all_to_all(made.reshape(experts, held, D), 'dp', split_axis=0, concat...  55.3 us
    dot_general x8, matrix products, mm(): lax.dot_general(a, b, (contract, ((), ())), preferred_element_type=jnp.fl...  32.9 us
    all_gather x1, waiting for transfers between devices, shards_rows(): lax.all_gather(jnp.concatenate([w_in[0], w_exp_out[0], extra], axis=0), '...  24 us
    all_to_all x2, waiting for transfers between devices, to_block(): return lax.all_to_all(split, 'seq', split_axis=0, concat_axis=0, tiled=True)  22.8 us
  transfers between devices with their start and end apart: 11, of which 10 were waited for; matrix products, arithmetic and copies ran while one was open for 13% of the time, Pallas kernels for 0%

profile of v2, /device:TPU:0, one launch (start us, length us, event | category | flops | bytes accessed | tf_op | source)
XLA Modules:
  0.0 721.8 jit_solution(9450111094044703158)
XLA Ops:
  36.6 7.3 %all-to-all-done = bf16[4,144,768]{2,1,0:T(8,128)(2,1)S(1)} async-done(((bf16[4,144,768]{2,1,0:T(8,128)(2,1)}), bf16[4,144,768]{2,1,0:T(8,128)(2,1)S(1)}, u32[]{:S(2)}, u32[]{:S(2)}) %all-to-all-start) | async-done | bytes 884768 | tf_op jit(solution)/shard_map/all_to_all | solution.py:568
  43.9 8.1 %all-to-all-start.4 = ((bf16[8,160,768]{2,1,0:T(8,128)(2,1)}), bf16[8,160,768]{2,1,0:T(8,128)(2,1)}, u32[]{:S(2)}, u32[]{:S(2)}) async-start(bf16[8,160,768]{2,1,0:T(8,128)(2,1)} %bitcast.25), calls=%async_computation.4 | async-start | bytes 3932160 | tf_op jit(solution)/shard_map/all_to_all | solution.py:628
  52.8 56.6 %all-gather.4.cloned.1.call-done = bf16[768,3200]{1,0:T(8,128)(2,1)} async-done(((bf16[24,3200]{1,0:T(8,128)(2,1)}), bf16[768,3200]{1,0:T(8,128)(2,1)}) %all-gather.4.cloned.1.call-update) | async-done | bytes 4915216 | tf_op jit(solution)/shard_map/all_gather | solution.py:604
  111.7 5.0 convolution_convert_fusion
  123.2 9.7 %fusion.72 = (f32[12,576]{1,0:T(8,128)S(1)}, f32[12,576,576]{1,2,0:T(8,128)}) fusion(pred[576]{0:T(1024)(128)(4,1)S(1)} %compare_reduce_fusion, bf16[576,12,64]{0,2,1:T(8,128)(2,1)S(1)} %bitcast.118, bf16[576,12,64]{0,2,1:T(8,128)(2,1)S(1)} %bitcast.116), kind=kOutput, calls=%fused_computation.134 | convolution fusion | flops 525533760 | bytes 17722944 | tf_op jit(solution)/shard_map/sub | solution.py:642
  132.9 8.0 %fusion.29 = bf16[12,64,576]{2,1,0:T(8,128)(2,1)S(1)} fusion(bf16[576,12,64]{0,2,1:T(8,128)(2,1)} %bitcast.130, f32[12,576,576]{1,2,0:T(8,128)} %get-tuple-element.168, f32[12,576]{1,0:T(8,128)S(1)} %get-tuple-element.167), kind=kOutput, calls=%fused_computation.66 | convolution fusion | flops 518012928 | bytes 17722368 | tf_op jit(solution)/shard_map/hqk,khd->qhd/dot_general | solution.py:645
  148.0 24.0 %all-gather.6.cloned.1.call-done = bf16[6208,768]{1,0:T(8,128)(2,1)} async-done(((bf16[1552,768]{1,0:T(8,128)(2,1)}), bf16[6208,768]{1,0:T(8,128)(2,1)}) %all-gather.6.cloned.1.call-update) | async-done | bytes 9535504 | tf_op jit(solution)/shard_map/all_gather | solution.py:613
  173.4 4.4 all-to-all-start.3
  179.2 8.0 %fusion.69 = (bf16[4,768,768]{2,1,0:T(8,128)(2,1)}, bf16[4,768,768]{2,1,0:T(8,128)(2,1)}) fusion(bf16[4,1552,768]{2,1,0:T(8,128)(2,1)} %bitcast.115), kind=kLoop, calls=%fused_computation.131 | loop fusion | bytes 18874368 | tf_op jit(solution)/shard_map/slice | solution.py:616
  190.5 99.6 %moe.1 = (bf16[576,768]{1,0:T(8,128)(2,1)}, bf16[1280,768]{1,0:T(8,128)(2,1)}, bf16[4,768,768]{2,1,0:T(8,128)(2,1)}, bf16[4,768,768]{2,1,0:T(8,128)(2,1)}, f32[7...) custom-call(bf16[576,768]{1,0:T(8,128)(2,1)} %bitcast.22.h_ref, bf16[1280,576]{1,0:T(8,128)(2,1)} %fusion.15.into_ref, ...), custom_call_target="tpu_custom_call" | custom-call | flops 36238786560 | bytes 40000000 | tf_op jit(solution)/shard_map/moe/pallas_call | solution.py:505
  290.2 17.0 %all_to_all.70 = bf16[4,144,768]{2,1,0:T(8,128)(2,1)} all-to-all(bf16[4,144,768]{2,1,0:T(8,128)(2,1)} %bitcast.138), channel_id=1, replica_groups=mesh['dp'=8,'seq'=4] {'seq'}, dimensions={0} | all-to-all | bytes 1769472 | tf_op jit(solution)/shard_map/all_to_all | solution.py:568
  317.0 7.2 all-to-all-done.6
  332.4 11.5 %multiply_reduce_fusion = (f32[12,576]{1,0:T(8,128)S(1)}, f32[12,576,576]{1,2,0:T(8,128)}) fusion(f32[12,576,576]{1,2,0:T(8,128)} %get-tuple-element.168, f32[12,576]{1,0:T(8,128)S(1)} %get-tuple-element.167, bf16[576,12,64]{0,2,1:T(8,128)(2,1)S(1)} %bitcast.132, bf16[576,12,64]{0,2,1:T(8,128)(2,1)S(1)} %bitcast.131), kind=kOutput, calls=%fused_computation.2 | convolution fusion | flops 521544960 | bytes 33675264 | tf_op jit(solution)/shard_map/qhd,khd->hqk/dot_general | solution.py:685
  343.9 12.1 %multiply_convert_fusion = bf16[12,576,576]{1,2,0:T(8,128)(2,1)S(1)} fusion(f32[12,576,576]{1,2,0:T(8,128)} %get-tuple-element.170, f32[12,576]{1,0:T(8,128)S(1)} %get-tuple-element.169, f32[12,576,576]{1,2,0:T(8,128)} %get-tuple-element.168, f32[12,576]{1,0:T(8,128)S(1)} %get-tuple-element.167), kind=kLoop, calls=%fused_computation.1 | loop fusion | flops 15925248 | bytes 39868416 | tf_op jit(solution)/shard_map/convert_element_type | solution.py:687
  360.5 8.9 %fusion.32 = bf16[12,64,576]{2,1,0:T(8,128)(2,1)S(1)} fusion(bf16[576,12,64]{0,2,1:T(8,128)(2,1)S(1)} %bitcast.133, f32[12,576,576]{1,2,0:T(8,128)} %get-tuple-element.168, f32[12,576]{1,0:T(8,128)S(1)} %get-tuple-element.167), kind=kOutput, calls=%fused_computation.67 | convolution fusion | flops 518012928 | bytes 17722368 | tf_op jit(solution)/shard_map/hqk,qhd->khd/dot_general | solution.py:690
  371.9 7.3 %fusion.37 = f32[768,2304]{1,0:T(8,128)} fusion(bf16[576,768]{1,0:T(8,128)(2,1)S(1)} %copy-done.15, bf16[576,768]{0,1:T(8,128)(2,1)S(1)} %bitcast.150, bf16[576,768]{0,1:T(8,128)(2,1)S(1)} %bitcast.134, bf16[576,768]{0,1:T(8,128)(2,1)S(1)} %bitcast.122), kind=kOutput, calls=%fused_computation.69 | convolution fusion | flops 2046394368 | bytes 10616832 | tf_op jit(solution)/shard_map/dot_general | solution.py:547
  387.4 11.8 %concatenate.27 = f32[768,3200]{1,0:T(8,128)} concatenate(f32[768,2304]{1,0:T(8,128)} %fusion.37, f32[768,768]{1,0:T(8,128)} %fusion.63, f32[768,1]{1,0:T(8,128)S(1)} %stack.48, f32[768,1]{1,0:T(8,128)S(1)} %stack.49, f32[768,1]{1,0:T(8,128)} %stack.50, f32[768,1]{1,0:T(8,128)} %stack.51, f32[768,1]{1,0:T(8,128)} %stack.52, f32[768,8]{1,0:T(8,128)} %bitcast.139, ...), dimensions={1} | concatenate | bytes 19660800 | tf_op jit(solution)/shard_map/concatenate | solution.py:705
  401.2 7.7 %pad_maximum_fusion = bf16[4,1552,768]{2,1,0:T(8,128)(2,1)} fusion(bf16[4,16,768]{2,1,0:T(8,128)(2,1)S(1)} %scatter.19, bf16[4,768,768]{2,1,0:T(8,128)(2,1)} %get-tuple-element.73, bf16[4,768,768]{2,1,0:T(8,128)(2,1)} %get-tuple-element.72), kind=kLoop, calls=%fused_computation.6 | loop fusion | flops 28606464 | bytes 19070976 | tf_op jit(solution)/shard_map/concatenate | solution.py:668
  416.3 19.5 %all-to-all-done.2 = bf16[4,144,768]{2,1,0:T(8,128)(2,1)} async-done(((bf16[4,144,768]{2,1,0:T(8,128)(2,1)}), bf16[4,144,768]{2,1,0:T(8,128)(2,1)}, u32[]{:S(2)}, u32[]{:S(2)}) %all-to-all-start.2) | async-done | bytes 884768 | tf_op jit(solution)/shard_map/all_to_all | solution.py:573
  435.8 16.9 %all_to_all.71 = bf16[4,144,768]{2,1,0:T(8,128)(2,1)S(1)} all-to-all(bf16[4,144,768]{2,1,0:T(8,128)(2,1)} %bitcast.121), channel_id=1, replica_groups=mesh['dp'=8,'seq'=4] {'seq'}, dimensions={0} | all-to-all | bytes 1769472 | tf_op jit(solution)/shard_map/all_to_all | solution.py:573
  452.7 7.2 all-to-all-start.5
  462.7 55.3 %all-to-all-done.5 = bf16[8,160,768]{2,1,0:T(8,128)(2,1)S(1)} async-done(((bf16[8,160,768]{2,1,0:T(8,128)(2,1)}), bf16[8,160,768]{2,1,0:T(8,128)(2,1)S(1)}, u32[]{:S(2)}, u32[]{:S(2)}) %all-to-all-start.5) | async-done | bytes 1966112 | tf_op jit(solution)/shard_map/all_to_all | solution.py:656
  522.0 103.9 %all-reduce.7.cloned.1.call-done = f32[768,3200]{1,0:T(8,128)} async-done(((f32[768,3200]{1,0:T(8,128)}), f32[768,3200]{1,0:T(8,128)}) %all-reduce.7.cloned.1.call-update) | async-done | bytes 9830416
  632.2 75.5 %reduce-scatter.2.cloned.1.call-done = bf16[1,1552,768]{2,1,0:T(8,128)(2,1)} async-done(((bf16[4,1552,768]{2,1,0:T(8,128)(2,1)}), bf16[1,1552,768]{2,1,0:T(8,128)(2,1)}) %reduce-scatter.2.cloned.1.call-update) | async-done | bytes 2383888 | tf_op jit(solution)/shard_map/reduce_scatter | solution.py:667
  (164 shorter events, 114.7 us)
Async XLA Ops:
  7.2 102.2 %all-gather.4.cloned.1.call-start = ((), (), s32[]{:S(2)}) async-start(), calls=%async_computation.10 | async-start | bytes 5068800 | tf_op jit(solution)/shard_map/all_gather | solution.py:604
  13.4 158.6 %all-gather.6.cloned.1.call-start = ((), (), s32[]{:S(2)}) async-start(), calls=%async_computation.12 | async-start | bytes 11919360 | tf_op jit(solution)/shard_map/all_gather | solution.py:613
  18.9 12.4 %copy-start.13 = (bf16[4,144,768]{2,1,0:T(8,128)(2,1)S(1)}, bf16[4,144,768]{2,1,0:T(8,128)(2,1)}, u32[]{:S(2)}) copy-start(bf16[4,144,768]{2,1,0:T(8,128)(2,1)} %param.26) | copy-start | bytes 2654212
  19.5 8.2 %all-to-all-start.1 = ((s32[4,8,144]{2,1,0:T(8,128)}), s32[4,8,144]{2,1,0:T(8,128)S(1)}, u32[]{:S(2)}, u32[]{:S(2)}) async-start(s32[4,8,144]{2,1,0:T(8,128)} %broadcast_in_dim.35), calls=%async_computation.1 | async-start | bytes 65536 | tf_op jit(solution)/shard_map/all_to_all | solution.py:632
  25.0 9.5 %copy-start.17 = (s32[576]{0:T(1024)}, s32[576]{0:T(1024)S(1)}, u32[]{:S(2)}) copy-start(s32[576]{0:T(1024)S(1)} %get-tuple-element.150) | copy-start | bytes 6916
  25.0 9.5 %copy-start.19 = (s32[576]{0:T(1024)}, s32[576]{0:T(1024)S(1)}, u32[]{:S(2)}) copy-start(s32[576]{0:T(1024)S(1)} %get-tuple-element.151) | copy-start | bytes 6916
  27.7 16.2 %all-to-all-start = ((bf16[4,144,768]{2,1,0:T(8,128)(2,1)}), bf16[4,144,768]{2,1,0:T(8,128)(2,1)S(1)}, u32[]{:S(2)}, u32[]{:S(2)}) async-start(bf16[4,144,768]{2,1,0:T(8,128)(2,1)} %param.25), calls=%async_computation | async-start | bytes 1769472 | tf_op jit(solution)/shard_map/all_to_all | solution.py:568
  43.9 129.5 %all-to-all-start.4 = ((bf16[8,160,768]{2,1,0:T(8,128)(2,1)}), bf16[8,160,768]{2,1,0:T(8,128)(2,1)}, u32[]{:S(2)}, u32[]{:S(2)}) async-start(bf16[8,160,768]{2,1,0:T(8,128)(2,1)} %bitcast.25), calls=%async_computation.4 | async-start | bytes 3932160 | tf_op jit(solution)/shard_map/all_to_all | solution.py:628
  118.7 14.2 %copy-start.6 = (bf16[576,768]{0,1:T(8,128)(2,1)}, bf16[576,768]{0,1:T(8,128)(2,1)S(1)}, u32[]{:S(2)}) copy-start(bf16[576,768]{0,1:T(8,128)(2,1)S(1)} %copy.107) | copy-start | bytes 2654212
  120.6 12.3 %copy-start.4 = (bf16[576,768]{0,1:T(8,128)(2,1)}, bf16[576,768]{0,1:T(8,128)(2,1)S(1)}, u32[]{:S(2)}) copy-start(bf16[576,768]{0,1:T(8,128)(2,1)S(1)} %copy.108) | copy-start | bytes 2654212
  173.4 17.1 %all-to-all-start.3 = ((bf16[4,144,768]{2,1,0:T(8,128)(2,1)}), bf16[4,144,768]{2,1,0:T(8,128)(2,1)}, u32[]{:S(2)}, u32[]{:S(2)}) async-start(bf16[4,144,768]{2,1,0:T(8,128)(2,1)} %bitcast.120), calls=%async_computation.3 | async-start | bytes 1769472 | tf_op jit(solution)/shard_map/all_to_all | solution.py:573
  307.2 17.0 %all-to-all-start.6 = ((bf16[4,144,768]{2,1,0:T(8,128)(2,1)}), bf16[4,144,768]{2,1,0:T(8,128)(2,1)}, u32[]{:S(2)}, u32[]{:S(2)}) async-start(bf16[4,144,768]{2,1,0:T(8,128)(2,1)} %param.26), calls=%async_computation.6 | async-start | bytes 1769472 | tf_op jit(solution)/shard_map/all_to_all | solution.py:568
  311.4 314.6 %all-reduce.7.cloned.1.call-start = ((), (), s32[]{:S(2)}) async-start(), calls=%async_computation.13 | async-start | bytes 19660800
  332.4 11.5 %copy-start.11 = (bf16[576,768]{0,1:T(8,128)(2,1)}, bf16[576,768]{0,1:T(8,128)(2,1)S(1)}, u32[]{:S(2)}) copy-start(bf16[576,768]{0,1:T(8,128)(2,1)S(1)} %copy.111) | copy-start | bytes 2654212
  343.9 12.1 %copy-start.5 = (bf16[576,768]{0,1:T(8,128)(2,1)S(1)}, bf16[576,768]{0,1:T(8,128)(2,1)}, u32[]{:S(2)}) copy-start(bf16[576,768]{0,1:T(8,128)(2,1)} %copy-done.4) | copy-start | bytes 2654212
  357.7 21.5 %slice-start = ((s8[4915200]{0:T(1024)(128)(4,1)}), s8[4194304]{0:T(1024)(128)(4,1)S(1)}, s32[]{:S(2)}) async-start(s8[4915200]{0:T(1024)(128)(4,1)} %bitcast.142), calls=%async_computation.14 | async-start | bytes 8388608
  360.4 8.9 %copy-start.3 = (f32[576,768]{1,0:T(8,128)S(1)}, f32[576,768]{1,0:T(8,128)}, u32[]{:S(2)}) copy-start(f32[576,768]{1,0:T(8,128)} %copy-done.2) | copy-start | bytes 5308420
  360.5 8.9 %copy-start.9 = (bf16[12,64,576]{2,1,0:T(8,128)(2,1)S(1)}, bf16[12,64,576]{2,1,0:T(8,128)(2,1)}, u32[]{:S(2)}) copy-start(bf16[12,64,576]{2,1,0:T(8,128)(2,1)} %copy-done.8) | copy-start | bytes 2654212
  360.5 18.8 %slice-start.1 = ((s8[4915200]{0:T(1024)(128)(4,1)}), s8[720896]{0:T(1024)(128)(4,1)S(1)}, s32[]{:S(2)}) async-start(s8[4915200]{0:T(1024)(128)(4,1)} %bitcast.142), calls=%async_computation.15 | async-start | bytes 1441792
  399.2 308.5 %reduce-scatter.2.cloned.1.call-start = ((), (), s32[]{:S(2)}) async-start(), calls=%async_computation.11 | async-start | bytes 11919360 | tf_op jit(solution)/shard_map/reduce_scatter | solution.py:667
  409.0 26.8 %all-to-all-start.2 = ((bf16[4,144,768]{2,1,0:T(8,128)(2,1)}), bf16[4,144,768]{2,1,0:T(8,128)(2,1)}, u32[]{:S(2)}, u32[]{:S(2)}) async-start(bf16[4,144,768]{2,1,0:T(8,128)(2,1)} %bitcast.137), calls=%async_computation.2 | async-start | bytes 1769472 | tf_op jit(solution)/shard_map/all_to_all | solution.py:573
  452.7 65.3 %all-to-all-start.5 = ((bf16[8,160,768]{2,1,0:T(8,128)(2,1)}), bf16[8,160,768]{2,1,0:T(8,128)(2,1)S(1)}, u32[]{:S(2)}, u32[]{:S(2)}) async-start(bf16[8,160,768]{2,1,0:T(8,128)(2,1)} %bitcast.124), calls=%async_computation.5 | async-start | bytes 3932160 | tf_op jit(solution)/shard_map/all_to_all | solution.py:656
  459.9 58.1 %copy-start.18 = (s32[576]{0:T(1024)S(1)}, s32[576]{0:T(1024)}, u32[]{:S(2)}) copy-start(s32[576]{0:T(1024)} %copy-done.17) | copy-start | bytes 6916
  459.9 58.1 %copy-start.20 = (s32[576]{0:T(1024)S(1)}, s32[576]{0:T(1024)}, u32[]{:S(2)}) copy-start(s32[576]{0:T(1024)} %copy-done.19) | copy-start | bytes 6916
  (12 other events, 39.6 us)
Sparse Core Ops, SparseCore 0:
  13.5 95.7 all-gather.3
  110.9 61.0 all-gather.5
  399.3 226.5 all-reduce.6
  628.6 79.0 reduce-scatter.1

commit v3 on v2

--- a/solution.py
+++ b/solution.py
@@ -370,8 +370,7 @@
     first_grad_ref,
     second_grad_ref,
     router_grad_ref,
-    bias1_grad_ref,
-    bias2_grad_ref,
+    bias_grad_ref,
     sent,
     rows,
     rows_t,
@@ -481,10 +480,10 @@
     def _(q):
         first_grad_ref[q] = nn(rows_t[...], gp[q]).astype(bf)
         second_grad_ref[q] = tn(act[q], go[...]).astype(bf)
-        bias1_grad_ref[q] = nn(ones, gp[q])
-
-    bias2_grad_ref[...] = nn(ones, go[...])
-    router_grad_ref[...] = nn(rows_t[...], logit_grad[...])
+        bias_grad_ref[q, :8] = nn(ones, gp[q])
+        bias_grad_ref[q, 8:] = nn(ones, go[...])
+
+    router_grad_ref[...] = tn(logit_grad[...], rows[...])[: router_grad_ref.shape[0]]
 
     @pl.loop(1, n)
     def _(step):
@@ -509,12 +508,11 @@
             sds(big, bf),
             sds(first.shape, bf),
             sds(second.shape, bf),
-            sds((width, 128), f32),
-            sds((blocks, 8, hidden), f32),
             sds((8, width), f32),
+            sds((blocks, 16, hidden), f32),
         ),
         in_specs=[VMEM] * 4 + [ANY] * 2 + [VMEM] * 3,
-        out_specs=(VMEM,) * 7,
+        out_specs=(VMEM,) * 6,
         scratch_shapes=[
             pltpu.VMEM(big, bf),
             pltpu.VMEM(big, bf),
@@ -561,6 +559,564 @@
         scaled
         - jnp.mean(scaled, axis=-1, keepdims=True)
         - normed * jnp.mean(scaled * normed, axis=-1, keepdims=True)
+    )
+
+
+def rows_of(i, size):
+    return pl.ds(pl.multiple_of(i * size, size), size)
+
+
+def split_axes():
+    dp, seq = lax.axis_index("dp"), lax.axis_index("seq")
+    return dp // 2, lax.rem(dp, 2), seq // 2, lax.rem(seq, 2)
+
+
+def greet(n_dp, n_seq):
+    dp, seq = lax.axis_index("dp"), lax.axis_index("seq")
+    barrier = pltpu.get_barrier_semaphore()
+    for step in range(1, n_dp):
+        pl.semaphore_signal(
+            barrier, inc=1, device_id=(other(dp, step), seq), device_id_type=MESH
+        )
+    for step in range(1, n_seq):
+        pl.semaphore_signal(
+            barrier, inc=1, device_id=(dp, lax.rem(seq + step, n_seq)), device_id_type=MESH
+        )
+    pl.semaphore_wait(barrier, n_dp - 1 + n_seq - 1)
+
+
+def remote(source, target, send, recv, device):
+    return pltpu.make_async_remote_copy(
+        source, target, send, recv, device_id=device, device_id_type=MESH
+    )
+
+
+def back_kernel(
+    n_dp,
+    n_seq,
+    grad_any,
+    resid_any,
+    x_any,
+    dy_any,
+    att_any,
+    qkv_any,
+    probs_any,
+    packed_any,
+    vectors_ref,
+    outs_any,
+    outof_any,
+    tokens_any,
+    branch_any,
+    first_any,
+    second_any,
+    bias_ref,
+    router_grad_ref,
+    block_out_ref,
+    tokens_grad_ref,
+    dense_ref,
+    small_ref,
+    expert_ref,
+    bias_out_ref,
+    grad_rows,
+    resid,
+    x_row,
+    dy_row,
+    att,
+    qkv,
+    probs,
+    w_qkv,
+    w_out,
+    outs,
+    outof,
+    tokens,
+    branch,
+    own_e,
+    recv_e,
+    recv_x,
+    recv_b,
+    grad_resid,
+    grad_att,
+    grad_qkv,
+    h_one,
+    grad_x,
+    part,
+    recv_c,
+    recv_1,
+    recv_2,
+    recv_3,
+    sums,
+    recv_s,
+    load_sem,
+    probs_sem,
+    own_sem,
+    gs_sem,
+    gr_sem,
+    os_sem,
+    or_sem,
+    es_sem,
+    er_sem,
+    xs_sem,
+    xr_sem,
+    bs_sem,
+    br_sem,
+    ps_sem,
+    pr_sem,
+    ss_sem,
+    sr_sem,
+    ts_sem,
+    tr_sem,
+):
+    bf, f32 = jnp.bfloat16, jnp.float32
+    dp, seq = lax.axis_index("dp"), lax.axis_index("seq")
+    z, y, x, c = split_axes()
+    pos = grad_rows.shape[0] // n_seq
+    cap = outs.shape[0] // n_dp
+    core_peer, x_peer = (dp, x * 2 + 1 - c), (dp, (1 - x) * 2 + c)
+    y_peer = (z * 2 + 1 - y, seq)
+    z_peer = lambda step: (lax.rem(z + step, 4) * 2 + y, seq)
+    loads = [
+        pltpu.make_async_copy(a, b, load_sem.at[i])
+        for i, (a, b) in enumerate(
+            (
+                (resid_any, resid),
+                (dy_any, dy_row),
+                (att_any, att),
+                (packed_any.at[:, 3 * D : 4 * D], w_out),
+                (qkv_any, qkv),
+                (x_any, x_row),
+                (packed_any.at[:, : 3 * D], w_qkv),
+                (outof_any, outof),
+                (tokens_any, tokens),
+                (branch_any, branch),
+            )
+        )
+    ]
+    fetch = lambda head: pltpu.make_async_copy(
+        probs_any.at[head], probs.at[head % 2], probs_sem.at[head % 2]
+    )
+    for load in loads[:4]:
+        load.start()
+    greet(n_dp, n_seq)
+    to_rows = []
+    for step in range(1, n_seq):
+        to = lax.rem(seq + step, n_seq)
+        to_rows.append(
+            remote(
+                grad_any.at[rows_of(to, pos)],
+                grad_rows.at[rows_of(seq, pos)],
+                gs_sem.at[step],
+                gr_sem.at[step],
+                (dp, to),
+            )
+        )
+    for copy in to_rows:
+        copy.start()
+    own_rows = pltpu.make_async_copy(
+        grad_any.at[rows_of(seq, pos)], grad_rows.at[rows_of(seq, pos)], own_sem.at[0]
+    )
+    own_rows.start()
+    experts_c, experts_own = [], []
+    for i, side in enumerate((1 - x, x)):
+        for j, ref in enumerate((first_any, second_any)):
+            k = i * 2 + j
+            experts_c.append(
+                remote(
+                    ref.at[side * 2 + 1 - c],
+                    recv_e.at[i, j],
+                    es_sem.at[k],
+                    er_sem.at[k],
+                    core_peer,
+                )
+            )
+            experts_own.append(
+                pltpu.make_async_copy(ref.at[side * 2 + c], own_e.at[i, j], own_sem.at[1 + k])
+            )
+    for copy in experts_c + experts_own:
+        copy.start()
+    returns = []
+    for step in range(n_dp - 1, 0, -1):
+        to = other(dp, step)
+        returns.append(
+            remote(
+                outs_any.at[rows_of(to, cap)],
+                outs.at[rows_of(dp, cap)],
+                os_sem.at[step],
+                or_sem.at[step],
+                (to, seq),
+            )
+        )
+    for copy in returns:
+        copy.start()
+    own_outs = pltpu.make_async_copy(
+        outs_any.at[rows_of(dp, cap)], outs.at[rows_of(dp, cap)], own_sem.at[5]
+    )
+    own_outs.start()
+    biases = []
+    for step in range(1, n_seq):
+        to = lax.rem(seq + step, n_seq)
+        biases.append(
+            remote(bias_ref.at[to], recv_b.at[step], bs_sem.at[step], br_sem.at[step], (dp, to))
+        )
+    for copy in biases:
+        copy.start()
+    for load in loads[4:]:
+        load.start()
+    fetch(0).start()
+    fetch(1).start()
+    vec = lambda i: vectors_ref[i : i + 1, :]
+    row_sum = lambda v: jnp.sum(v, axis=0, keepdims=True)
+
+    def norm_back(grad_output, values, gain):
+        normed, inv = norm_stats(values)
+        sums_of = (row_sum(grad_output * normed), row_sum(grad_output))
+        return norm_grad(grad_output, normed, inv, gain), *sums_of
+
+    def piece_fill(i, value):
+        half = value.shape[1] // 2
+        for owner in range(n_dp * n_seq):
+            oz, oy, ox, oc = owner // 8, owner // 4 % 2, owner // 2 % 2, owner % 2
+            block = value[24 * owner : 24 * owner + 24].astype(bf)
+            part[i, oc, 0, ox, oy, oz] = block[:, :half]
+            part[i, oc, 1, oy, ox, oz] = block[:, half:]
+
+    first_axis = ((x, x_peer), (y, y_peer))
+
+    def piece_copies(i, stage):
+        sems = lambda k: (ps_sem.at[i, k], pr_sem.at[i, k])
+        if stage == 0:
+            return [remote(part.at[i, 1 - c], recv_c.at[i], *sems(0), core_peer)]
+        made = []
+        for h in range(2):
+            (f, f_peer), (g, g_peer) = first_axis[h], first_axis[1 - h]
+            if stage == 1:
+                made.append(
+                    remote(part.at[i, c, h, 1 - f], recv_1.at[i, h], *sems(1 + h), f_peer)
+                )
+            elif stage == 2:
+                made.append(
+                    remote(part.at[i, c, h, f, 1 - g], recv_2.at[i, h], *sems(3 + h), g_peer)
+                )
+            else:
+                for step in range(1, 4):
+                    made.append(
+                        remote(
+                            part.at[i, c, h, f, g, lax.rem(z + step, 4)],
+                            recv_3.at[i, h, step],
+                            *sems(4 + h * 3 + step),
+                            z_peer(step),
+                        )
+                    )
+        return made
+
+    def add(a, b):
+        return (a.astype(f32) + b.astype(f32)).astype(bf)
+
+    def piece_advance(i, stage):
+        for copy in piece_copies(i, stage - 1):
+            copy.wait_recv()
+        if stage == 1:
+            part[i, c] = add(part[i, c], recv_c[i])
+        for h in range(2):
+            f, g = first_axis[h][0], first_axis[1 - h][0]
+            if stage == 2:
+                part[i, c, h, f] = add(part[i, c, h, f], recv_1[i, h])
+            elif stage == 3:
+                part[i, c, h, f, g] = add(part[i, c, h, f, g], recv_2[i, h])
+            elif stage == 4:
+                total = part[i, c, h, f, g, z].astype(f32)
+                for step in range(1, 4):
+                    total = total + recv_3[i, h, step].astype(f32)
+                half = total.shape[1]
+                dense_ref[:, (2 * i + h) * half : (2 * i + h + 1) * half] = total
+        if stage < 4:
+            for copy in piece_copies(i, stage):
+                copy.start()
+
+    def small_copies(stage):
+        peers = ([core_peer], [x_peer], [y_peer], [z_peer(1), z_peer(2), z_peer(3)])[stage]
+        return [
+            remote(
+                sums.at[stage],
+                recv_s.at[stage + k],
+                ss_sem.at[stage + k],
+                sr_sem.at[stage + k],
+                peer,
+            )
+            for k, peer in enumerate(peers)
+        ]
+
+    def small_advance(stage):
+        for copy in small_copies(stage - 1):
+            copy.wait_recv()
+        if stage < 4:
+            sums[stage] = sums[stage - 1] + recv_s[stage - 1]
+            for copy in small_copies(stage):
+                copy.start()
+        else:
+            small_ref[...] = sums[3] + recv_s[3] + recv_s[4] + recv_s[5]
+
+    own_e_copies = experts_own
+
+    def experts_send_x():
+        for j in range(2):
+            experts_c[j].wait_recv()
+            own_e_copies[j].wait()
+            own_e[0, j] = add(own_e[0, j], recv_e[0, j])
+            experts_x[j].start()
+
+    experts_x = [
+        remote(own_e.at[0, j], recv_x.at[j], xs_sem.at[j], xr_sem.at[j], x_peer) for j in range(2)
+    ]
+
+    def experts_end():
+        for j in range(2):
+            experts_c[2 + j].wait_recv()
+            own_e_copies[2 + j].wait()
+            experts_x[j].wait_recv()
+
+            @pl.loop(0, 6)
+            def _(k):
+                at = rows_of(k, recv_x.shape[1] // 6)
+                expert_ref[j, at, :] = (
+                    own_e[1, j, at, :].astype(f32)
+                    + recv_e[1, j, at, :].astype(f32)
+                    + recv_x[j, at, :].astype(f32)
+                )
+
+        bias = bias_ref[seq]
+        for step in range(1, n_seq):
+            biases[step - 1].wait_recv()
+            bias = bias + recv_b[step]
+        bias_out_ref[...] = bias
+
+    for load in loads[:3]:
+        load.wait()
+    own_rows.wait()
+    for copy in to_rows:
+        copy.wait_recv()
+    grad_in, gain_two, shift_two = norm_back(grad_rows[...].astype(f32), resid[...], vec(3))
+    grad_resid[...] = dy_row[...].astype(f32) + grad_in
+    grad_branch = grad_resid[...].astype(bf)
+    out_shift = row_sum(grad_branch.astype(f32))
+    loads[3].wait()
+    grad_att[...] = nt(grad_branch, w_out[...]).astype(bf)
+    piece_fill(0, tn(att[...], grad_branch))
+    for copy in piece_copies(0, 0):
+        copy.start()
+    loads[4].wait()
+    loads[5].wait()
+    x_normed, _ = norm_stats(x_row[...].astype(f32))
+    h_one[...] = (x_normed * vec(0) + vec(1)).astype(bf)
+    experts_send_x()
+    lane = lax.broadcasted_iota(jnp.int32, (1, 128), 1) // HEAD
+    scale = HEAD ** (-0.5)
+    for pair in range(HEADS // 2):
+        cols = slice(128 * pair, 128 * pair + 128)
+        q, k, v = (qkv[:, D * i + 128 * pair : D * i + 128 * pair + 128] for i in range(3))
+        go = grad_att[:, cols]
+        both = go.astype(f32) * att[:, cols].astype(f32)
+        grads = [jnp.zeros(q.shape, f32)] * 3
+        for h in range(2):
+            head = 2 * pair + h
+            keep = (lane == h).astype(bf)
+            fetch(head).wait()
+            p = probs[head % 2]
+            go_h = go * keep
+            delta = jnp.sum(both * keep.astype(f32), axis=-1, keepdims=True)
+            ds = (p.astype(f32) * (nt(go_h, v) - delta)).astype(bf)
+            grads = [
+                grads[0] + nn(ds, k * keep),
+                grads[1] + tn(ds, q * keep),
+                grads[2] + tn(p, go_h),
+            ]
+            if head + 2 < HEADS:
+                fetch(head + 2).start()
+        for i, factor in enumerate((scale, scale, 1.0)):
+            at = (2 * 128) * (3 * (pair // 2) + i) + 128 * (pair % 2)
+            grad_qkv[:, at : at + 128] = (grads[i] * factor).astype(bf)
+        if pair < 4:
+            piece_advance(0, pair + 1)
+        if pair in (2, 3, 4, 5):
+            piece_advance(1, pair - 1)
+        if pair in (4, 5):
+            piece_advance(2, pair - 3)
+        if pair % 2 == 1:
+            i = pair // 2 + 1
+            piece_fill(i, tn(h_one[...], grad_qkv[:, D * (i - 1) : D * i]))
+            for copy in piece_copies(i, 0):
+                copy.start()
+    loads[6].wait()
+    grad_h1 = jnp.zeros(resid.shape, f32)
+    for i in range(9):
+        at = 256 * i
+        col = D * (i % 3) + 256 * (i // 3)
+        grad_h1 = grad_h1 + nt(grad_qkv[:, at : at + 256], w_qkv[:, col : col + 256])
+    grad_in, gain_one, shift_one = norm_back(grad_h1, x_row[...].astype(f32), vec(0))
+    sums[0] = jnp.concatenate(
+        [gain_one, shift_one, out_shift, gain_two, shift_two, jnp.zeros((3, D), f32), router_grad_ref[...]], axis=0
+    )
+    for copy in small_copies(0):
+        copy.start()
+    grad_x[...] = (grad_resid[...] + grad_in).astype(bf)
+    to_blocks = []
+    for step in range(1, n_seq):
+        to = lax.rem(seq + step, n_seq)
+        to_blocks.append(
+            remote(
+                grad_x.at[rows_of(to, pos)],
+                tokens_grad_ref.at[rows_of(seq, pos)],
+                ts_sem.at[step],
+                tr_sem.at[step],
+                (dp, to),
+            )
+        )
+    for copy in to_blocks:
+        copy.start()
+    tokens_grad_ref[rows_of(seq, pos), :] = grad_x[rows_of(seq, pos), :]
+    piece_advance(3, 1)
+    piece_advance(2, 3)
+    small_advance(1)
+    own_outs.wait()
+    for copy in returns:
+        copy.wait_recv()
+    for load in loads[7:]:
+        load.wait()
+    block_out_ref[...] = (
+        tokens[...].astype(f32) + branch[...].astype(f32) + nn(outof[...], outs[...])
+    ).astype(bf)
+    piece_advance(3, 2)
+    small_advance(2)
+    piece_advance(2, 4)
+    experts_end()
+    piece_advance(3, 3)
+    small_advance(3)
+    piece_advance(3, 4)
+    small_advance(4)
+    for copy in to_blocks:
+        copy.wait_recv()
+    for copy in to_rows + experts_c + returns + biases + experts_x + to_blocks:
+        copy.wait_send()
+    for stage in range(4):
+        for i in range(4):
+            for copy in piece_copies(i, stage):
+                copy.wait_send()
+        for copy in small_copies(stage):
+            copy.wait_send()
+
+
+def back(
+    n_dp,
+    n_seq,
+    grad_h2,
+    resid,
+    x_row,
+    dy_row,
+    att,
+    qkv,
+    probs,
+    packed,
+    vectors,
+    outs,
+    outof,
+    tokens,
+    branch,
+    first_grad,
+    second_grad,
+    biases,
+    router_grad,
+):
+    bf, f32 = jnp.bfloat16, jnp.float32
+    sds, dma, vmem = jax.ShapeDtypeStruct, pltpu.SemaphoreType.DMA, pltpu.VMEM
+    tok, slots = outof.shape
+    pos = tok // n_seq
+    half = D // 2
+    return pl.pallas_call(
+        functools.partial(back_kernel, n_dp, n_seq),
+        out_shape=(
+            sds((tok, D), bf),
+            sds((tok, D), bf),
+            sds((D // (n_dp * n_seq), 4 * D), f32),
+            sds((16, D), f32),
+            sds((2,) + first_grad.shape[1:], f32),
+            sds(biases.shape[1:], f32),
+        ),
+        in_specs=[ANY] * 8 + [VMEM] + [ANY] * 6 + [VMEM] * 2,
+        out_specs=(VMEM,) * 6,
+        scratch_shapes=[
+            vmem((tok, D), bf),
+            vmem((tok, D), f32),
+            vmem((tok, D), bf),
+            vmem((tok, D), bf),
+            vmem((tok, D), bf),
+            vmem((tok, 3 * D), bf),
+            vmem((2,) + probs.shape[1:], bf),
+            vmem((D, 3 * D), bf),
+            vmem((D, D), bf),
+            vmem((slots, D), bf),
+            vmem((tok, slots), bf),
+            vmem((tok, D), bf),
+            vmem((tok, D), bf),
+            vmem((2, 2, D, D), bf),
+            vmem((2, 2, D, D), bf),
+            vmem((2, D, D), bf),
+            vmem((n_seq,) + biases.shape[1:], f32),
+            vmem((tok, D), f32),
+            vmem((tok, D), bf),
+            vmem((tok, 3 * D), bf),
+            vmem((tok, D), bf),
+            vmem((tok, D), bf),
+            vmem((4, 2, 2, 2, 2, 4, 24, half), bf),
+            vmem((4, 2, 2, 2, 4, 24, half), bf),
+            vmem((4, 2, 2, 4, 24, half), bf),
+            vmem((4, 2, 4, 24, half), bf),
+            vmem((4, 2, 4, 24, half), bf),
+            vmem((4, 16, D), f32),
+            vmem((6, 16, D), f32),
+            dma((10,)),
+            dma((2,)),
+            dma((6,)),
+            dma((n_seq,)),
+            dma((n_seq,)),
+            dma((n_dp,)),
+            dma((n_dp,)),
+            dma((4,)),
+            dma((4,)),
+            dma((2,)),
+            dma((2,)),
+            dma((n_seq,)),
+            dma((n_seq,)),
+            dma((4, 11)),
+            dma((4, 11)),
+            dma((6,)),
+            dma((6,)),
+            dma((n_seq,)),
+            dma((n_seq,)),
+        ],
+        compiler_params=pltpu.CompilerParams(
+            collective_id=2, has_side_effects=True, vmem_limit_bytes=61 * 2**20
+        ),
+        cost_estimate=pl.CostEstimate(
+            flops=10**10, bytes_accessed=5 * 10**7, transcendentals=10**6
+        ),
+        name="back",
+    )(
+        grad_h2,
+        resid,
+        x_row,
+        dy_row,
+        att,
+        qkv,
+        probs,
+        packed,
+        vectors,
+        outs,
+        outof,
+        tokens,
+        branch,
+        first_grad,
+        second_grad,
+        biases,
+        router_grad,
     )
 
 
@@ -606,7 +1162,7 @@
     )
     qkv_weight, out_weight = packed[:, : 3 * D], packed[:, 3 * D : 4 * D]
     vectors = packed[:, 4 * D : 4 * D + 5].T.astype(f32)
-    gain_one, shift_one, out_shift, gain_two, shift_two = (v[None] for v in vectors)
+    gain_one, shift_one, out_shift, gain_two, shift_two = (vectors[i : i + 1] for i in range(5))
     router = packed[:, 4 * D + 5 : 4 * D + 5 + experts]
     bias_cols = exp_out_bias.shape[1]
     extra = jnp.zeros((16, D), bf).at[0].set(in_bias[0]).at[1, :bias_cols].set(exp_out_bias[0])
@@ -627,12 +1183,12 @@
     dy_slots = mm(into, cotangent.reshape(tok, D), ((1,), (0,)), True).reshape(experts, held, D)
     dy_slots = lax.all_to_all(dy_slots, "dp", split_axis=0, concat_axis=0, tiled=True)
     dy_slots = dy_slots.reshape(-1, D)
-    x = to_row(tokens).astype(f32)
-    dy = to_row(cotangent).astype(f32)
+    x_low, dy = to_row(tokens), to_row(cotangent)
+    x = x_low.astype(f32)
     open_row = lax.all_to_all(
         jnp.broadcast_to(pad_mask[:, None], (rows_dev, 8, pos_dev)), "seq", 0, 2, tiled=True
     )[0, :1]
-    normed_one, inv_one = norm_stats(x)
+    normed_one, _ = norm_stats(x)
     h_one = (normed_one * gain_one + shift_one).astype(bf)
     qkv = mm(h_one, qkv_weight, ((1,), (0,)), True)
     q, k, v = (qkv[:, i * D : (i + 1) * D].reshape(-1, HEADS, HEAD) for i in range(3))
@@ -645,84 +1201,56 @@
     attended = jnp.einsum("hqk,khd->qhd", probs_low, v, preferred_element_type=f32)
     attended = attended.astype(bf).reshape(-1, D)
     branch = mm(attended, out_weight, ((1,), (0,))) + out_shift
-    normed_two, inv_two = norm_stats(x + branch)
+    resid = x + branch
+    normed_two, _ = norm_stats(resid)
     h_two = (normed_two * gain_two + shift_two).astype(bf)
     h_block = to_block(h_two, rows_dev).reshape(tok, D)
     branch_block = to_block(branch.astype(bf), rows_dev).reshape(tok, D)
     wide_router = jnp.pad(router, ((0, 0), (0, 128 - experts)))
-    grad_h2, made, first_grad, second_grad, router_grad, bias1_grad, bias2_grad = moe(
+    grad_h2, made, first_grad, second_grad, router_grad, bias_grad = moe(
         h_block, into, outof, dy_slots, first, second, first_bias[:, None], second_bias, wide_router, experts
     )
-    made = lax.all_to_all(
-        made.reshape(experts, held, D),
-        "dp",
-        split_axis=0,
-        concat_axis=0,
-        tiled=True,
-    ).reshape(-1, D)
-    extra = jnp.zeros((n_seq, 16, D), f32).at[:, 0].set(bias1_grad[:, 0])
-    extra = extra.at[:, 1, :bias_cols].set(bias2_grad[0].reshape(n_seq, bias_cols))
-    extra = extra.astype(bf)
-    router_grad = router_grad[:, :experts]
-    expert_grads = lax.psum_scatter(
-        jnp.concatenate([first_grad, second_grad, extra], axis=1),
-        "seq",
-        scatter_dimension=0,
-    ).astype(f32)
-    block_output = (
-        tokens.reshape(tok, D).astype(f32)
-        + branch_block.astype(f32)
-        + mm(outof, made, ((1,), (0,)))
-    ).astype(bf)
-    grad_h2 = to_row(grad_h2.reshape(rows_dev, pos_dev, D)).astype(f32)
-    gain_two_grad = jnp.sum(grad_h2 * normed_two, axis=0)
-    shift_two_grad = jnp.sum(grad_h2, axis=0)
-    grad_resid = dy + norm_grad(grad_h2, normed_two, inv_two, gain_two)
-    grad_branch = grad_resid.astype(bf)
-    out_weight_grad = mm(attended, grad_branch, ((0,), (0,)))
-    out_shift_grad = jnp.sum(grad_branch, axis=0, dtype=f32)
-    grad_att = mm(grad_branch, out_weight, ((1,), (1,)), True).reshape(-1, HEADS, HEAD)
-    grad_probs = jnp.einsum("qhd,khd->hqk", grad_att, v, preferred_element_type=f32)
-    delta = jnp.sum(probs * grad_probs, axis=-1, keepdims=True)
-    grad_scores = (probs * (grad_probs - delta)).astype(bf)
-    grad_q = jnp.einsum("hqk,khd->qhd", grad_scores, k, preferred_element_type=f32) * scale
-    grad_k = jnp.einsum("hqk,qhd->khd", grad_scores, q, preferred_element_type=f32) * scale
-    grad_v = jnp.einsum("hqk,qhd->khd", probs_low, grad_att, preferred_element_type=f32)
-    grad_qkv = jnp.concatenate(
-        [g.astype(bf).reshape(-1, D) for g in (grad_q, grad_k, grad_v)], axis=1
-    )
-    qkv_weight_grad = mm(h_one, grad_qkv, ((0,), (0,)))
-    grad_h1 = mm(grad_qkv, qkv_weight, ((1,), (1,)))
-    gain_one_grad = jnp.sum(grad_h1 * normed_one, axis=0)
-    shift_one_grad = jnp.sum(grad_h1, axis=0)
-    grad_x = (grad_resid + norm_grad(grad_h1, normed_one, inv_one, gain_one)).astype(bf)
-    tokens_grad = to_block(grad_x, rows_dev)
-    vectors = jnp.stack(
-        [gain_one_grad, shift_one_grad, out_shift_grad, gain_two_grad, shift_two_grad], axis=1
-    )
-    pad = jnp.zeros((D, 128 - 5 - experts), f32)
-    dense = lax.psum_scatter(
-        jnp.concatenate([qkv_weight_grad, out_weight_grad, vectors, router_grad, pad], axis=1),
-        both,
-        scatter_dimension=0,
-        tiled=True,
-    )
-    vectors = dense[:, 4 * D : 4 * D + 5].T
+    out, tokens_grad, dense, small, expert_grads, bias_grad = back(
+        lax.axis_size("dp"),
+        n_seq,
+        grad_h2,
+        resid,
+        x_low,
+        dy,
+        attended,
+        qkv,
+        probs_low,
+        packed,
+        jnp.pad(vectors, ((0, 3), (0, 0))),
+        made,
+        outof,
+        tokens.reshape(tok, D),
+        branch_block,
+        first_grad,
+        second_grad,
+        bias_grad,
+        router_grad,
+    )
+    seq, own = lax.axis_index("seq"), D // (lax.axis_size("dp") * n_seq)
+    small = lax.dynamic_slice_in_dim(
+        small, (lax.axis_index("dp") * n_seq + seq) * own, own, 1
+    )
+    qkv_grad = dense[:, D:].reshape(own, 3, 3, 256).swapaxes(1, 2).reshape(own, 3 * D)
     return (
-        block_output.reshape(rows_dev, pos_dev, D),
-        tokens_grad,
-        vectors[0],
-        vectors[1],
-        dense[:, : 3 * D],
-        dense[:, 3 * D : 4 * D],
-        vectors[2],
-        vectors[3],
-        vectors[4],
-        dense[:, 4 * D + 5 : 4 * D + 5 + experts],
-        expert_grads[None, :D],
-        expert_grads[None, 2 * D],
-        expert_grads[None, D : 2 * D],
-        expert_grads[None, 2 * D + 1, :bias_cols],
+        out.reshape(rows_dev, pos_dev, D),
+        tokens_grad.reshape(rows_dev, pos_dev, D),
+        small[0],
+        small[1],
+        qkv_grad,
+        dense[:, :D],
+        small[2],
+        small[3],
+        small[4],
+        small[8 : 8 + experts].T,
+        expert_grads[None, 0],
+        bias_grad[None, 0],
+        expert_grads[None, 1],
+        lax.dynamic_slice_in_dim(bias_grad[None, 8], seq * bias_cols, bias_cols, 1),
     )
 
 

time: 728 us -> 438 us (0.60)
  waiting for transfers between devices: 354 us -> 68.2 us
  Pallas kernels: 99.6 us -> 234 us
  matrix products: 75.9 us -> 26.2 us
  blocking collectives: 33.9 us -> 0 us
  other arithmetic: 48.9 us -> 18.8 us
  local copies, waits for them, and re-layouts: 59.1 us -> 46.1 us
  starting transfers between devices: 36 us -> 24.1 us
    pallas_call x0 -> x1, Pallas kernels: none -> 134 us  [back(): pl.pallas_call(functools.partial(back_kernel, n_dp, n_seq), out_shape=(sd...]
    unnamed x5 -> x2, waiting for transfers between devices: 104 us -> 0.03 us
    reduce_scatter x1 -> x0, waiting for transfers between devices: 75.5 us -> none  [shards_rows(): lax.psum_scatter(jnp.concatenate([first_grad, second_grad, extra], axis=1...]
    all_to_all x1 -> x0, waiting for transfers between devices: 55.3 us -> none  [shards_rows(): lax.all_to_all(made.reshape(experts, held, D), 'dp', split_axis=0, concat...]
    all_to_all x2 -> x0, blocking collectives: 33.9 us -> none  [the longest x1 17 us: to_row(): lax.all_to_all(block, 'seq', split_axis=0, concat_axis=1, tiled=True)[0]]
    dot_general x4 -> x0, matrix products: 24.8 us -> none  [the longest x1 11.5 us: shards_rows(): jnp.einsum('qhd,khd->hqk', grad_att, v, preferred_element_type=f32)]
    all_gather x1, waiting for transfers between devices: 56.6 us -> 31.8 us  [shards_rows(): lax.all_gather(jnp.concatenate([w_qkv, w_out, vectors, w_router, pad], ax...]
    dot_general x8 -> x3, matrix products: 32.9 us -> 12.2 us  [mm(): lax.dot_general(a, b, (contract, ((), ())), preferred_element_type=jnp.fl...]
  transfers between devices with their start and end apart: 11 -> 8, of which waited for: 10 -> 6; matrix products, arithmetic and copies ran while one was open for 13% -> 15% of each run, Pallas kernels for 0% -> 23%
where the time goes in v3:
time: 438 us; the launch traced here: 432 us
  Pallas kernels  234 us (53%)
  waiting for transfers between devices  68.2 us (16%)
  local copies, waits for them, and re-layouts  46.1 us (11%)
  matrix products  26.2 us (6%)
  starting transfers between devices  24.1 us (6%)
  other arithmetic  18.8 us (4%)
  between operations  14.5 us (3%)
    pallas_call x1, Pallas kernels, back(): pl.pallas_call(functools.partial(back_kernel, n_dp, n_seq), out_shape=(sd...  134 us
    pallas_call x1, Pallas kernels, moe(): pl.pallas_call(functools.partial(moe_kernel, experts), out_shape=(sds((to...  100 us
    all_gather x1, waiting for transfers between devices, shards_rows(): lax.all_gather(jnp.concatenate([w_qkv, w_out, vectors, w_router, pad], ax...  31.8 us
    all_gather x1, waiting for transfers between devices, shards_rows(): lax.all_gather(jnp.concatenate([w_in[0], w_exp_out[0], extra], axis=0), '...  18.6 us
    dot_general x3, matrix products, mm(): lax.dot_general(a, b, (contract, ((), ())), preferred_element_type=jnp.fl...  12.2 us
    sub x1, matrix products, shards_rows(): weights = jnp.exp(scores - jnp.max(scores, axis=-1, keepdims=True))  10.9 us
  transfers between devices with their start and end apart: 8, of which 6 were waited for; matrix products, arithmetic and copies ran while one was open for 15% of the time, Pallas kernels for 23%

profile of v3, /device:TPU:0, one launch (start us, length us, event | category | flops | bytes accessed | tf_op | source)
XLA Modules:
  0.0 432.3 jit_solution(974307396735753785)
XLA Ops:
  14.9 3.2 pad_maximum_fusion
  19.4 4.2 all-to-all-start.1
  27.7 3.5 all-to-all-start
  31.2 4.4 %convolution_convert_fusion.1 = bf16[1280,768]{1,0:T(8,128)(2,1)} fusion(bf16[576,768]{1,0:T(8,128)(2,1)} %bitcast.22, s32[576]{0:T(1024)S(1)} %get-tuple-element.70, s32[576]{0:T(1024)S(1)} %get-tuple-element.69), kind=kOutput, calls=%fused_computation.10 | convolution fusion | flops 1135656960 | bytes 2855424 | tf_op jit(solution)/shard_map/dot_general | solution.py:545
  35.6 2.0 fusion.10.into_ref
  37.8 6.1 %all-to-all-done = bf16[4,144,768]{2,1,0:T(8,128)(2,1)S(1)} async-done(((bf16[4,144,768]{2,1,0:T(8,128)(2,1)}), bf16[4,144,768]{2,1,0:T(8,128)(2,1)S(1)}, u32[]{:S(2)}, u32[]{:S(2)}) %all-to-all-start) | async-done | bytes 884768 | tf_op jit(solution)/shard_map/all_to_all | solution.py:1124
  43.9 4.4 %all-to-all-start.4 = ((bf16[4,144,768]{2,1,0:T(8,128)(2,1)}), bf16[4,144,768]{2,1,0:T(8,128)(2,1)}, u32[]{:S(2)}, u32[]{:S(2)}) async-start(bf16[4,144,768]{2,1,0:T(8,128)(2,1)} %param.22), calls=%async_computation.4 | async-start | bytes 1769472 | tf_op jit(solution)/shard_map/all_to_all | solution.py:1124
  49.2 31.8 %all-gather.4.cloned.1.call-done.packed_any = bf16[768,3200]{1,0:T(8,128)(2,1)} async-done(((bf16[24,3200]{1,0:T(8,128)(2,1)}), bf16[768,3200]{1,0:T(8,128)(2,1)}) %all-gather.4.cloned.1.call-update) | async-done | bytes 4915216 | tf_op jit(solution)/shard_map/all_gather | solution.py:1160
  82.8 4.4 %convolution_convert_fusion.qkv_any = bf16[576,2304]{1,0:T(8,128)(2,1)S(1)} fusion(bf16[768,3200]{1,0:T(8,128)(2,1)} %all-gather.4.cloned.1.call-done.packed_any, bf16[576,768]{1,0:T(8,128)(2,1)S(1)} %bitcast.81, f32[768]{0:T(1024)S(1)} %get-tuple-element.65, f32[768]{0:T(1024)S(1)} %get-tuple-element.66, f32[576]{0:T(1024)S(1)} %rsqrt.20, f32[576]{0:T(1024)S(1)} %div.23), kind=kOutput, calls=%fused_computation.8 | convolution fusion | flops 2042413056 | bytes 7088640 | tf_op jit(solution)/shard_map/dot_general | solution.py:545
  89.1 2.3 copy.76
  93.3 10.9 %fusion.56 = (f32[12,576]{1,0:T(8,128)S(1)}, f32[12,576,576]{2,1,0:T(8,128)}) fusion(pred[576]{0:T(1024)(128)(4,1)S(1)} %compare_reduce_fusion, bf16[576,12,64]{0,2,1:T(8,128)(2,1)} %bitcast.90, bf16[576,12,64]{0,2,1:T(8,128)(2,1)} %bitcast.91), kind=kOutput, calls=%fused_computation.96 | convolution fusion | flops 525533760 | bytes 17722944 | tf_op jit(solution)/shard_map/sub | solution.py:1198
  104.2 4.4 %all-to-all-start.3 = ((bf16[8,160,768]{2,1,0:T(8,128)(2,1)}), bf16[8,160,768]{2,1,0:T(8,128)(2,1)}, u32[]{:S(2)}, u32[]{:S(2)}) async-start(bf16[8,160,768]{2,1,0:T(8,128)(2,1)} %bitcast.86), calls=%async_computation.3 | async-start | bytes 3932160 | tf_op jit(solution)/shard_map/all_to_all | solution.py:1184
  108.6 7.0 %divide_convert_fusion.probs_any = bf16[12,576,576]{2,1,0:T(8,128)(2,1)S(1)} fusion(f32[12,576,576]{2,1,0:T(8,128)} %get-tuple-element.88, f32[12,576]{1,0:T(8,128)S(1)} %get-tuple-element.87), kind=kLoop, calls=%fused_computation.1 | loop fusion | flops 7962624 | bytes 23915520 | tf_op jit(solution)/shard_map/convert_element_type | solution.py:1200
  115.6 2.7 convolution_convert_fusion.2
  120.4 3.4 add_convert_fusion.1
  127.6 18.6 %all-gather.6.cloned.1.call-done = bf16[6208,768]{1,0:T(8,128)(2,1)} async-done(((bf16[1552,768]{1,0:T(8,128)(2,1)}), bf16[6208,768]{1,0:T(8,128)(2,1)}) %all-gather.6.cloned.1.call-update) | async-done | bytes 9535504 | tf_op jit(solution)/shard_map/all_gather | solution.py:1169
  147.7 7.0 %all-to-all-done.3 = bf16[8,160,768]{2,1,0:T(8,128)(2,1)} async-done(((bf16[8,160,768]{2,1,0:T(8,128)(2,1)}), bf16[8,160,768]{2,1,0:T(8,128)(2,1)}, u32[]{:S(2)}, u32[]{:S(2)}) %all-to-all-start.3) | async-done | bytes 1966112 | tf_op jit(solution)/shard_map/all_to_all | solution.py:1184
  154.7 4.0 all-to-all-start.2
  160.1 7.9 %fusion.52 = (bf16[4,768,768]{2,1,0:T(8,128)(2,1)}, bf16[4,768,768]{2,1,0:T(8,128)(2,1)}) fusion(bf16[4,1552,768]{2,1,0:T(8,128)(2,1)} %bitcast.80), kind=kLoop, calls=%fused_computation.92 | loop fusion | bytes 18874368 | tf_op jit(solution)/shard_map/slice | solution.py:1172
  168.0 3.4 all-to-all-done.2
  171.3 3.5 all-to-all-start.5
  174.9 100.1 %moe.1 = (bf16[576,768]{1,0:T(8,128)(2,1)}, bf16[1280,768]{1,0:T(8,128)(2,1)}, bf16[4,768,768]{2,1,0:T(8,128)(2,1)}, bf16[4,768,768]{2,1,0:T(8,128)(2,1)}, f32[8,768]{1,0:T(8,128)}, /*index=5*/f32[4,16,768]{2,1,0:T(8,128)}) custom-call(bf16[576,768]{1,0:T(8,128)(2,1)} %bitcast.95, bf16[1280,576]{1,0:T(8,128)(2,1)} %fusion.10.into_ref, ...), custom_call_target="tpu_custom_call" | custom-call | flops 36238786560 | bytes 40000000 | tf_op jit(solution)/shard_map/moe/pallas_call | solution.py:504
  275.9 134.2 %back.1 = (bf16[576,768]{1,0:T(8,128)(2,1)}, bf16[576,768]{1,0:T(8,128)(2,1)}, f32[24,3072]{1,0:T(8,128)}, f32[16,768]{1,0:T(8,128)}, f32[2,768,768]{2,1,0:T(8,128)}, /*index=5*/f32[16,768]{1,0:T(8,128)}) custom-call(bf16[576,768]{1,0:T(8,128)(2,1)} %get-tuple-element.50.grad_any, f32[576,768]{1,0:T(8,128)} %copy-done.1, bf16[576,768]{1,0:T(8,128)(2,1)} %bitcast.82, ...), custom_call_target="tpu_custom_call" | custom-call | flops 10000000000 | bytes 50000000 | tf_op jit(solution)/shard_map/back/pallas_call | solution.py:1033
  412.6 4.9 %fusion.53 = (f32[1,768,768]{2,1,0:T(8,128)}, f32[1,768,768]{2,1,0:T(8,128)}) fusion(f32[2,768,768]{2,1,0:T(8,128)} %get-tuple-element.60), kind=kLoop, calls=%fused_computation.93 | loop fusion | bytes 9437184 | tf_op jit(solution)/shard_map/slice | solution.py:1252
  (99 shorter events, 39.3 us)
Async XLA Ops:
  7.2 73.9 %all-gather.4.cloned.1.call-start = ((), (), s32[]{:S(2)}) async-start(), calls=%async_computation.6 | async-start | bytes 5068800 | tf_op jit(solution)/shard_map/all_gather | solution.py:1160
  13.4 132.9 %all-gather.6.cloned.1.call-start = ((), (), s32[]{:S(2)}) async-start(), calls=%async_computation.7 | async-start | bytes 11919360 | tf_op jit(solution)/shard_map/all_gather | solution.py:1169
  18.1 0.7 copy-start.9
  18.1 5.5 %copy-start.10 = (s32[4,144,2]{1,2,0:T(2,128)S(1)}, s32[4,144,2]{1,2,0:T(2,128)}, u32[]{:S(2)}) copy-start(s32[4,144,2]{1,2,0:T(2,128)} %param.24) | copy-start | bytes 13828
  18.1 5.7 %copy-start.11 = (s32[4,144]{1,0:T(4,128)S(1)}, s32[4,144]{1,0:T(4,128)}, u32[]{:S(2)}) copy-start(s32[4,144]{1,0:T(4,128)} %param.25) | copy-start | bytes 6916
  19.4 8.3 %all-to-all-start.1 = ((s32[4,8,144]{2,1,0:T(8,128)}), s32[4,8,144]{2,1,0:T(8,128)S(1)}, u32[]{:S(2)}, u32[]{:S(2)}) async-start(s32[4,8,144]{2,1,0:T(8,128)} %broadcast_in_dim.33), calls=%async_computation.1 | async-start | bytes 65536 | tf_op jit(solution)/shard_map/all_to_all | solution.py:1188
  27.7 16.2 %all-to-all-start = ((bf16[4,144,768]{2,1,0:T(8,128)(2,1)}), bf16[4,144,768]{2,1,0:T(8,128)(2,1)S(1)}, u32[]{:S(2)}, u32[]{:S(2)}) async-start(bf16[4,144,768]{2,1,0:T(8,128)(2,1)} %param.21), calls=%async_computation | async-start | bytes 1769472 | tf_op jit(solution)/shard_map/all_to_all | solution.py:1124
  43.9 76.5 %copy-start.2 = (bf16[4,144,768]{2,1,0:T(8,128)(2,1)}, bf16[4,144,768]{2,1,0:T(8,128)(2,1)S(1)}, u32[]{:S(2)}) copy-start(bf16[4,144,768]{2,1,0:T(8,128)(2,1)S(1)} %all-to-all-done) | copy-start | bytes 2654212
  43.9 60.2 %all-to-all-start.4 = ((bf16[4,144,768]{2,1,0:T(8,128)(2,1)}), bf16[4,144,768]{2,1,0:T(8,128)(2,1)}, u32[]{:S(2)}, u32[]{:S(2)}) async-start(bf16[4,144,768]{2,1,0:T(8,128)(2,1)} %param.22), calls=%async_computation.4 | async-start | bytes 1769472 | tf_op jit(solution)/shard_map/all_to_all | solution.py:1124
  87.2 1.8 copy-start.4
  104.2 50.5 %all-to-all-start.3 = ((bf16[8,160,768]{2,1,0:T(8,128)(2,1)}), bf16[8,160,768]{2,1,0:T(8,128)(2,1)}, u32[]{:S(2)}, u32[]{:S(2)}) async-start(bf16[8,160,768]{2,1,0:T(8,128)(2,1)} %bitcast.86), calls=%async_computation.3 | async-start | bytes 3932160 | tf_op jit(solution)/shard_map/all_to_all | solution.py:1184
  115.6 3.4 copy-start
  119.0 1.4 copy-start.3
  123.8 3.8 copy-start.1
  154.7 16.6 %all-to-all-start.2 = ((bf16[4,144,768]{2,1,0:T(8,128)(2,1)}), bf16[4,144,768]{2,1,0:T(8,128)(2,1)S(1)}, u32[]{:S(2)}, u32[]{:S(2)}) async-start(bf16[4,144,768]{2,1,0:T(8,128)(2,1)} %bitcast.14), calls=%async_computation.2 | async-start | bytes 1769472 | tf_op jit(solution)/shard_map/all_to_all | solution.py:1129
  171.3 3.5 copy-start.8
  171.3 103.6 %all-to-all-start.5 = ((bf16[4,144,768]{2,1,0:T(8,128)(2,1)}), bf16[4,144,768]{2,1,0:T(8,128)(2,1)S(1)}, u32[]{:S(2)}, u32[]{:S(2)}) async-start(bf16[4,144,768]{2,1,0:T(8,128)(2,1)} %bitcast.31), calls=%async_computation.5 | async-start | bytes 1769472 | tf_op jit(solution)/shard_map/all_to_all | solution.py:1129
  275.0 0.9 copy-start.7
  412.6 10.8 %copy-start.6 = (bf16[576,768]{1,0:T(8,128)(2,1)S(1)}, bf16[576,768]{1,0:T(8,128)(2,1)}, u32[]{:S(2)}) copy-start(bf16[576,768]{1,0:T(8,128)(2,1)} %get-tuple-element.56) | copy-start | bytes 2654212
  417.5 6.8 %copy-start.5 = (bf16[576,768]{1,0:T(8,128)(2,1)S(1)}, bf16[576,768]{1,0:T(8,128)(2,1)}, u32[]{:S(2)}) copy-start(bf16[576,768]{1,0:T(8,128)(2,1)} %get-tuple-element.57) | copy-start | bytes 2654212
Sparse Core Ops, SparseCore 0:
  13.5 67.4 all-gather.3
  82.6 63.5 all-gather.5
